TPU v7x, 256 devices: a whole 4x4x8 slice. The times are simulated.
256 devices in a mesh: space: 64 (over y, z, core), coil: 4 (over x).
Axes of the slice: x: 4, y: 4, z: 8, core: 2. Of those that a mesh axis runs over, the one named last changes fastest.
Arguments:
- k_space: bfloat16 [2, 16, 256, 64, 320], P(None, 'coil', 'space'), may hold values from -6 to 6
- cotangent: bfloat16 [2, 16, 256, 64, 320], P(None, 'coil', 'space'), may hold values from -6 to 6
- sens_maps: bfloat16 [2, 16, 256, 64, 320], P(None, 'coil', None, 'space'), may hold values from -0.75 to 0.75
- line_index: int32 [256, 40], replicated, may hold values from 0 to 319, all different within a row
- w_first: bfloat16 [18, 2, 3, 3], replicated, may hold values from -1.5 to 1.5
- b_first: float32 [18], replicated, may hold values from -3 to 3
- w_second: bfloat16 [2, 18, 3, 3], replicated, may hold values from -0.5 to 0.5
- b_second: float32 [2], replicated, may hold values from -3 to 3
Outputs:
- grad_sens: bfloat16 [2, 16, 256, 64, 320], P(None, 'coil', None, 'space')
- grad_w1: float32 [18, 2, 3, 3], replicated
- grad_b1: float32 [18], replicated
- grad_w2: float32 [2, 18, 3, 3], replicated
- grad_b2: float32 [2], replicated
Inputs may be any that keep to these rules, and one draw needn't show every extreme that they name: Each row of line_index lists 40 different phase-encode indices.
All inputs are finite; a program needn't handle non-finite values.
Results may differ from a plain program's by a relative error of at most 0.04.
Values may be sent and summed in bfloat16 or wider, within the bound.
A program may use at most 320 MiB of HBM per device.

v0:
```python
import math

import jax
import jax.numpy as jnp
from jax import lax
from jax.sharding import PartitionSpec as P


def with_halo(cells, sides, width):
    for axis, dim in sides:
        count = lax.axis_size(axis)
        ends = count - 1
        head = lax.slice_in_dim(cells, 0, width, axis=dim)
        tail = lax.slice_in_dim(cells, cells.shape[dim] - width, cells.shape[dim], axis=dim)
        cells = jnp.concatenate(
            [
                lax.ppermute(tail, axis, [(i, (i + 1) % count) for i in range(ends)]),
                cells,
                lax.ppermute(head, axis, [((i + 1) % count, i) for i in range(ends)]),
            ],
            axis=dim,
        )
    return cells


def dft_table(length):
    position = jnp.arange(length, dtype=jnp.int32)
    product = position[:, None] * position[None, :] % length
    angles = 2.0 * math.pi / length * product.astype(jnp.float32)
    scaling = 1.0 / math.sqrt(length)
    cosine = jnp.cos(angles) * scaling
    sine_part = jnp.sin(angles) * scaling
    return jnp.stack([jnp.stack([cosine, sine_part]), jnp.stack([-sine_part, cosine])]).astype(
        jnp.bfloat16
    )


def plane_conv(padded, kernel):
    return lax.conv_general_dilated(
        padded,
        kernel,
        (1, 1),
        ((0, 0), (1, 1)),
        dimension_numbers=("CNHW", "OIHW", "CNHW"),
        preferred_element_type=jnp.float32,
    )


def flip_kernel(kernel):
    return jnp.transpose(kernel[:, :, ::-1, ::-1], (1, 0, 2, 3))


def kernel_grad(cot_array, padded):
    widened = jnp.pad(padded, ((0, 0), (0, 0), (0, 0), (1, 1)))
    len_x = cot_array.shape[2]
    len_y = cot_array.shape[3]
    row_list = []
    for shift_x in range(3):
        for shift_y in range(3):
            window = widened[:, :, shift_x : shift_x + len_x, shift_y : shift_y + len_y]
            row_list.append(
                jnp.einsum("ozxy,izxy->oi", cot_array, window, preferred_element_type=jnp.float32)
            )
    return jnp.stack(row_list, axis=2).reshape(cot_array.shape[0], padded.shape[0], 3, 3)


def regularize(combined, grad_reg, w_first, b_first, w_second, b_second, extend):
    comb_pad = extend(combined)
    hidden_pre = plane_conv(comb_pad, w_first) + b_first[:, None, None, None]
    activation = jax.nn.silu(hidden_pre).astype(jnp.bfloat16)
    act_pad = extend(activation)
    regularized = (plane_conv(act_pad, w_second) + b_second[:, None, None, None]).astype(
        jnp.bfloat16
    )
    grad_act = plane_conv(extend(grad_reg), flip_kernel(w_second))
    logistic = jax.nn.sigmoid(hidden_pre)
    grad_pre = (grad_act * logistic * (1.0 + hidden_pre * (1.0 - logistic))).astype(jnp.bfloat16)
    grad_comb = plane_conv(extend(grad_pre), flip_kernel(w_first)).astype(jnp.bfloat16)
    weight_grads = (
        kernel_grad(grad_pre, comb_pad),
        jnp.sum(grad_pre.astype(jnp.float32), axis=(1, 2, 3)),
        kernel_grad(grad_reg, act_pad),
        jnp.sum(grad_reg.astype(jnp.float32), axis=(1, 2, 3)),
    )
    return (regularized, grad_comb, weight_grads)


def with_rims(values):
    return with_halo(values, (("space", 2),), 1)


def run_regularizer(comb_image, back_cot, w_first, b_first, w_second, b_second):
    return regularize(comb_image, back_cot, w_first, b_first, w_second, b_second, with_rims)


def on_device(k_space, cotangent, sens_maps, line_index, w_first, b_first, w_second, b_second):
    n_space = lax.axis_size("space")
    local_z = k_space.shape[2]
    len_z = local_z * n_space
    len_y = k_space.shape[4]
    len_x = sens_maps.shape[3] * n_space
    table_y = dft_table(len_y)
    table_z = dft_table(len_z)
    own_lines = lax.dynamic_slice_in_dim(line_index, lax.axis_index("space") * local_z, local_z, 0)
    sampled = jnp.any(
        own_lines[:, :, None] == jnp.arange(len_y, dtype=jnp.int32)[None, None, :], axis=1
    ).astype(jnp.bfloat16)
    masked = k_space * sampled[None, None, :, None, :]
    arrived, cot_rows = (
        lax.all_to_all(masked, "space", split_axis=3, concat_axis=2, tiled=True),
        lax.all_to_all(cotangent, "space", split_axis=3, concat_axis=2, tiled=True),
    )
    half_image = jnp.einsum(
        "pczxk,pqky->qczxy", arrived, table_y, preferred_element_type=jnp.float32
    ).astype(jnp.bfloat16)
    half_back = jnp.einsum(
        "pczxk,pqky->qczxy", cot_rows, table_y, preferred_element_type=jnp.float32
    ).astype(jnp.bfloat16)
    coil_image = jnp.einsum(
        "pczxy,pqzw->qcwxy", half_image, table_z, preferred_element_type=jnp.float32
    ).astype(jnp.bfloat16)
    back_image = jnp.einsum(
        "pczxy,pqzw->qcwxy", half_back, table_z, preferred_element_type=jnp.float32
    ).astype(jnp.bfloat16)
    sens_f = sens_maps.astype(jnp.float32)
    image_f = coil_image.astype(jnp.float32)
    back_f = back_image.astype(jnp.float32)
    comb_part = jnp.stack(
        [
            jnp.sum(sens_f[0] * image_f[0] + sens_f[1] * image_f[1], axis=0),
            jnp.sum(sens_f[0] * image_f[1] - sens_f[1] * image_f[0], axis=0),
        ]
    )
    back_part = -jnp.stack(
        [
            jnp.sum(sens_f[0] * back_f[0] + sens_f[1] * back_f[1], axis=0),
            jnp.sum(sens_f[0] * back_f[1] - sens_f[1] * back_f[0], axis=0),
        ]
    )
    comb_total, back_total = lax.psum((comb_part, back_part), "coil")
    regularized, grad_comb, weight_grads = run_regularizer(
        comb_total.astype(jnp.bfloat16),
        back_total.astype(jnp.bfloat16),
        w_first,
        b_first,
        w_second,
        b_second,
    )
    first_w, first_b, second_w, second_b = weight_grads
    first_w, first_b, second_w, second_b = lax.psum((first_w, first_b, second_w, second_b), "space")
    scaling = 1.0 / math.sqrt(len_x * len_y * len_z)
    reg_f = regularized.astype(jnp.float32)[:, None]
    comb_grad_f = grad_comb.astype(jnp.float32)[:, None]
    real_part = (
        -(back_f[0] * reg_f[0] + back_f[1] * reg_f[1])
        + image_f[0] * comb_grad_f[0]
        + image_f[1] * comb_grad_f[1]
    )
    imag_part = (
        -(back_f[1] * reg_f[0] - back_f[0] * reg_f[1])
        + image_f[1] * comb_grad_f[0]
        - image_f[0] * comb_grad_f[1]
    )
    grad_sens = jnp.stack([real_part, imag_part]).astype(jnp.bfloat16)
    return (grad_sens, first_w * scaling, first_b * scaling, second_w * scaling, second_b * scaling)


def solution(mesh):
    placed = (
        P(None, "coil", "space", None, None),
        P(None, "coil", "space", None, None),
        P(None, "coil", None, "space", None),
        P(),
        P(),
        P(),
        P(),
        P(),
    )
    return jax.shard_map(
        on_device,
        mesh=mesh,
        in_specs=placed,
        out_specs=(P(None, "coil", None, "space", None), P(), P(), P(), P()),
        check_vma=False,
    )
```

profile of v0, /device:TPU:1, one launch (start us, length us, event | category | flops | bytes accessed | tf_op | source)
XLA Modules:
  0.0 526.4 jit_solution(5365733954020726359)
XLA Ops:
  1.7 3.8 copy_multiply_fusion
  5.5 13.2 %all-to-all-start.1 = ((bf16[2,4,4,64,320]{4,2,1,0,3:T(4,128)(2,1)}), bf16[2,4,4,64,320]{4,2,1,0,3:T(4,128)(2,1)S(1)}, u32[]{:S(2)}, u32[]{:S(2)}) async-start(bf16[2,4,4,64,320]{4,2,1,0,3:T(4,128)(2,1)} %copy_multiply_fusion), calls=%async_computation.1 | async-start | bytes 3145728 | tf_op jit(solution)/shard_map/all_to_all | solution.py:110
  18.7 2.4 copy.58
  21.1 37.4 %all-to-all-done.1 = bf16[2,4,4,64,320]{4,2,1,0,3:T(4,128)(2,1)S(1)} async-done(((bf16[2,4,4,64,320]{4,2,1,0,3:T(4,128)(2,1)}), bf16[2,4,4,64,320]{4,2,1,0,3:T(4,128)(2,1)S(1)}, u32[]{:S(2)}, u32[]{:S(2)}) %all-to-all-start.1) | async-done | bytes 1310752 | tf_op jit(solution)/shard_map/all_to_all | solution.py:110
  58.5 6.5 %all-to-all-start = ((bf16[2,4,4,64,320]{4,2,1,0,3:T(4,128)(2,1)}), bf16[2,4,4,64,320]{4,2,1,0,3:T(4,128)(2,1)S(1)}, u32[]{:S(2)}, u32[]{:S(2)}) async-start(bf16[2,4,4,64,320]{4,2,1,0,3:T(4,128)(2,1)} %copy.58), calls=%async_computation | async-start | bytes 3145728 | tf_op jit(solution)/shard_map/all_to_all | solution.py:111
  76.8 3.7 copy.66
  80.4 24.3 %all-to-all-done = bf16[2,4,4,64,320]{4,2,1,0,3:T(4,128)(2,1)S(1)} async-done(((bf16[2,4,4,64,320]{4,2,1,0,3:T(4,128)(2,1)}), bf16[2,4,4,64,320]{4,2,1,0,3:T(4,128)(2,1)S(1)}, u32[]{:S(2)}, u32[]{:S(2)}) %all-to-all-start) | async-done | bytes 1310752 | tf_op jit(solution)/shard_map/all_to_all | solution.py:111
  105.3 2.4 copy.60
  107.8 2.9 fusion.51
  119.1 31.0 %all-reduce.5 = (bf16[2,256,1,320]{1,0,3,2:T(2,128)(2,1)S(1)}, bf16[2,256,1,320]{1,0,3,2:T(2,128)(2,1)S(1)}) all-reduce(f32[2,256,1,320]{1,0,3,2:T(2,128)} %pad_maximum_fusion.2, f32[2,256,1,320]{1,0,3,2:T(2,128)} %maximum_negate_fusion), channel_id=1, replica_groups=mesh['space'=64,'coil'=4] {'coil'}, use_global_device_ids=true, to_apply=%region_3.4 | all-reduce | flops 327680 | bytes 1966080 | tf_op jit(solution)/shard_map/psum | solution.py:140
  150.2 6.6 %collective-permute-start.1 = (bf16[2,256,1,320]{1,0,3,2:T(2,128)(2,1)S(1)}, bf16[2,256,1,320]{1,0,3,2:T(2,128)(2,1)S(1)}, u32[]{:S(2)}, u32[]{:S(2)}) collective-permute-start(bf16[2,256,1,320]{1,0,3,2:T(2,128)(2,1)S(1)} %get-tuple-element.35), channel_id=1, source_target_pairs={{4,0},{8,4},{12,8},{16,12},{20,16},{24,20},{28,24},{32,28},{36,32}... | collective-permute-start | bytes 983048 | tf_op jit(solution)/shard_map/ppermute | solution.py:19
  156.8 2.8 collective-permute-start
  161.5 3.6 collective-permute-start.4
  166.0 5.4 %multiply_convert_fusion.1 = (bf16[18,256,1,320]{1,0,3,2:T(8,128)(2,1)S(1)}, f32[18,256,1,320]{1,0,3,2:T(8,128)}) fusion(f32[18]{0:T(128)S(1)} %copy-done.14, bf16[18,2,3,3]{0,1,3,2:T(2,128)(2,1)S(1)} %copy-done.12, bf16[2,256,1,320]{1,0,3,2:T(2,128)(2,1)S(1)} %collective-permute-done.1, bf16[2,256,1,320]{1,0,3,2:T(2,128)(2,1)S(1)} %get-tuple-element.35, ...), kind=kOutput, calls=%fused_computation.9 | convolution fusion | flops 64770048 | bytes 9831120 | tf_op jit(solution)/shard_map/conv_general_dilated | solution.py:39
  174.0 3.6 collective-permute-start.2
  177.7 6.8 %convert_reduce_fusion = (f32[18]{0:T(128)S(1)}, bf16[18,256,1,320]{1,0,3,2:T(8,128)(2,1)S(1)}) fusion(f32[18,256,1,320]{1,0,3,2:T(8,128)} %get-tuple-element.48, f32[18]{0:T(128)S(1)} %copy-done.14, bf16[2,18,3,3]{1,0,3,2:T(2,128)(2,1)S(1)} %copy-done.13, bf16[2,256,1,320]{1,0,3,2:T(2,128)(2,1)S(1)} %collective-permute-done.5, ...), kind=kOutput, calls=%fused_computation.7 | convolution fusion | flops 73617392 | bytes 9831192 | tf_op jit(solution)/shard_map/conv_general_dilated | solution.py:39
  187.1 3.6 collective-permute-start.6
  204.2 36.0 %collective-permute-done.7 = bf16[18,256,1,320]{1,3,2,0:T(8,128)(2,1)} collective-permute-done((bf16[18,256,1,320]{1,3,2,0:T(8,128)(2,1)S(1)}, bf16[18,256,1,320]{1,3,2,0:T(8,128)(2,1)}, u32[]{:S(2)}, u32[]{:S(2)}) %collective-permute-start.7) | collective-permute-done | bytes 2949152 | tf_op jit(solution)/shard_map/ppermute | solution.py:19
  240.3 3.6 copy.75
  245.9 4.8 fusion.61
  255.6 3.4 pad_maximum_fusion
  260.3 2.4 fusion.93
  273.0 5.8 %fusion.65 = f32[2,256,1,320]{1,0,3,2:T(2,128)} fusion(bf16[18,256,3,320]{1,0,3,2:T(8,128)(2,1)S(1)} %pad_maximum_fusion, bf16[2,18,3,3]{1,0,3,2:T(2,128)(2,1)S(1)} %copy-done.13, f32[2]{0:T(128)S(1)} %copy-done.15), kind=kOutput, calls=%fused_computation.82 | convolution fusion | flops 53465088 | bytes 9503376 | tf_op jit(solution)/shard_map/conv_general_dilated | solution.py:39
  278.8 241.0 %all-reduce.2 = (f32[18,2,3,3]{0,1,3,2:T(2,128)S(1)}, f32[18]{0:T(128)S(1)}, f32[2,18,3,3]{1,0,3,2:T(2,128)S(1)}, f32[2]{0:T(128)S(1)}) all-reduce(f32[18,2,3,3]{0,1,3,2:T(2,128)S(1)} %bitcast.280, f32[18]{0:T(128)S(1)} %get-tuple-element.49, f32[2,18,3,3]{1,0,3,2:T(2,128)S(1)} %bitcast.279, ...), channel_id=1, replica_groups=mesh['space'=64,'coil'=4] {'space'}, use_global_device_ids=true, to_apply=%region_7.8 | all-reduce | flops 668 | bytes 5344 | tf_op jit(solution)/shard_map/psum | solution.py:150
  (101 shorter events, 67.9 us)
Async XLA Ops:
  0.6 18.1 %copy-start.6 = (bf16[2,4,4,64,320]{4,3,2,1,0:T(8,128)(2,1)S(1)}, bf16[2,4,4,64,320]{4,3,2,1,0:T(8,128)(2,1)}, u32[]{:S(2)}) copy-start(bf16[2,4,4,64,320]{4,3,2,1,0:T(8,128)(2,1)} %param.9) | copy-start | bytes 3932164
  5.5 53.0 %all-to-all-start.1 = ((bf16[2,4,4,64,320]{4,2,1,0,3:T(4,128)(2,1)}), bf16[2,4,4,64,320]{4,2,1,0,3:T(4,128)(2,1)S(1)}, u32[]{:S(2)}, u32[]{:S(2)}) async-start(bf16[2,4,4,64,320]{4,2,1,0,3:T(4,128)(2,1)} %copy_multiply_fusion), calls=%async_computation.1 | async-start | bytes 3145728 | tf_op jit(solution)/shard_map/all_to_all | solution.py:110
  58.5 46.2 %all-to-all-start = ((bf16[2,4,4,64,320]{4,2,1,0,3:T(4,128)(2,1)}), bf16[2,4,4,64,320]{4,2,1,0,3:T(4,128)(2,1)S(1)}, u32[]{:S(2)}, u32[]{:S(2)}) async-start(bf16[2,4,4,64,320]{4,2,1,0,3:T(4,128)(2,1)} %copy.58), calls=%async_computation | async-start | bytes 3145728 | tf_op jit(solution)/shard_map/all_to_all | solution.py:111
  65.0 8.2 %copy-start.8 = (bf16[2,4,256,1,320]{2,4,3,1,0:T(8,128)(2,1)S(1)}, bf16[2,4,256,1,320]{2,4,3,1,0:T(8,128)(2,1)}, u32[]{:S(2)}) copy-start(bf16[2,4,256,1,320]{2,4,3,1,0:T(8,128)(2,1)} %param.10) | copy-start | bytes 3932164
  107.8 3.0 copy-start.7
  107.8 3.0 copy-start.10
  107.8 3.0 copy-start.11
  112.0 1.7 copy-start.4
  113.7 1.6 copy-start.2
  115.3 50.7 %copy-start.12 = (bf16[18,2,3,3]{0,1,3,2:T(2,128)(2,1)S(1)}, bf16[18,2,3,3]{0,1,3,2:T(2,128)(2,1)}, u32[]{:S(2)}) copy-start(bf16[18,2,3,3]{0,1,3,2:T(2,128)(2,1)} %param.12) | copy-start | bytes 1948
  115.3 50.7 %copy-start.14 = (f32[18]{0:T(128)S(1)}, f32[18]{0:T(128)}, u32[]{:S(2)}) copy-start(f32[18]{0:T(128)} %param.13) | copy-start | bytes 220
  150.2 15.8 %collective-permute-start.1 = (bf16[2,256,1,320]{1,0,3,2:T(2,128)(2,1)S(1)}, bf16[2,256,1,320]{1,0,3,2:T(2,128)(2,1)S(1)}, u32[]{:S(2)}, u32[]{:S(2)}) collective-permute-start(bf16[2,256,1,320]{1,0,3,2:T(2,128)(2,1)S(1)} %get-tuple-element.35), channel_id=1, source_target_pairs={{4,0},{8,4},{12,8},{16,12},{20,16},{24,20},{28,24},{32,28},{36,32}... | collective-permute-start | bytes 983048 | tf_op jit(solution)/shard_map/ppermute | solution.py:19
  156.8 9.2 %collective-permute-start = (bf16[2,256,1,320]{1,0,3,2:T(2,128)(2,1)S(1)}, bf16[2,256,1,320]{1,0,3,2:T(2,128)(2,1)S(1)}, u32[]{:S(2)}, u32[]{:S(2)}) collective-permute-start(bf16[2,256,1,320]{1,0,3,2:T(2,128)(2,1)S(1)} %get-tuple-element.35), channel_id=1, source_target_pairs={{0,4},{4,8},{8,12},{12,16},{16,20},{20,24},{24,28},{28,32},{32,36}... | collective-permute-start | bytes 983048 | tf_op jit(solution)/shard_map/ppermute | solution.py:17
  159.6 18.1 %collective-permute-start.5 = (bf16[2,256,1,320]{1,0,3,2:T(2,128)(2,1)S(1)}, bf16[2,256,1,320]{1,0,3,2:T(2,128)(2,1)S(1)}, u32[]{:S(2)}, u32[]{:S(2)}) collective-permute-start(bf16[2,256,1,320]{1,0,3,2:T(2,128)(2,1)S(1)} %get-tuple-element.36), channel_id=1, source_target_pairs={{4,0},{8,4},{12,8},{16,12},{20,16},{24,20},{28,24},{32,28},{36,32}... | collective-permute-start | bytes 983048 | tf_op jit(solution)/shard_map/ppermute | solution.py:19
  161.5 16.1 %collective-permute-start.4 = (bf16[2,256,1,320]{1,0,3,2:T(2,128)(2,1)S(1)}, bf16[2,256,1,320]{1,0,3,2:T(2,128)(2,1)S(1)}, u32[]{:S(2)}, u32[]{:S(2)}) collective-permute-start(bf16[2,256,1,320]{1,0,3,2:T(2,128)(2,1)S(1)} %get-tuple-element.36), channel_id=1, source_target_pairs={{0,4},{4,8},{8,12},{12,16},{16,20},{20,24},{24,28},{28,32},{32,36}... | collective-permute-start | bytes 983048 | tf_op jit(solution)/shard_map/ppermute | solution.py:17
  171.4 6.3 %copy-start.13 = (bf16[2,18,3,3]{1,0,3,2:T(2,128)(2,1)S(1)}, bf16[2,18,3,3]{1,0,3,2:T(2,128)(2,1)}, u32[]{:S(2)}) copy-start(bf16[2,18,3,3]{1,0,3,2:T(2,128)(2,1)} %param.14) | copy-start | bytes 1948
  172.1 81.7 %collective-permute-start.3 = (bf16[18,256,1,320]{1,3,2,0:T(8,128)(2,1)S(1)}, bf16[18,256,1,320]{1,3,2,0:T(8,128)(2,1)S(1)}, u32[]{:S(2)}, u32[]{:S(2)}) collective-permute-start(bf16[18,256,1,320]{1,3,2,0:T(8,128)(2,1)S(1)} %copy.68), channel_id=1, source_target_pairs={{4,0},{8,4},{12,8},{16,12},{20,16},{24,20},{28,24},{32,28},{36,32}... | collective-permute-start | bytes 8847368 | tf_op jit(solution)/shard_map/ppermute | solution.py:19
  174.0 78.0 %collective-permute-start.2 = (bf16[18,256,1,320]{1,3,2,0:T(8,128)(2,1)S(1)}, bf16[18,256,1,320]{1,3,2,0:T(8,128)(2,1)S(1)}, u32[]{:S(2)}, u32[]{:S(2)}) collective-permute-start(bf16[18,256,1,320]{1,3,2,0:T(8,128)(2,1)S(1)} %copy.68), channel_id=1, source_target_pairs={{0,4},{4,8},{8,12},{12,16},{16,20},{20,24},{24,28},{28,32},{32,36}... | collective-permute-start | bytes 8847368 | tf_op jit(solution)/shard_map/ppermute | solution.py:17
  185.2 55.1 %collective-permute-start.7 = (bf16[18,256,1,320]{1,3,2,0:T(8,128)(2,1)S(1)}, bf16[18,256,1,320]{1,3,2,0:T(8,128)(2,1)}, u32[]{:S(2)}, u32[]{:S(2)}) collective-permute-start(bf16[18,256,1,320]{1,3,2,0:T(8,128)(2,1)S(1)} %copy.72), channel_id=1, source_target_pairs={{4,0},{8,4},{12,8},{16,12},{20,16},{24,20},{28,24},{32,28},{36,32}... | collective-permute-start | bytes 8847368 | tf_op jit(solution)/shard_map/ppermute | solution.py:19
  187.1 56.7 %collective-permute-start.6 = (bf16[18,256,1,320]{1,3,2,0:T(8,128)(2,1)S(1)}, bf16[18,256,1,320]{1,3,2,0:T(8,128)(2,1)S(1)}, u32[]{:S(2)}, u32[]{:S(2)}) collective-permute-start(bf16[18,256,1,320]{1,3,2,0:T(8,128)(2,1)S(1)} %copy.72), channel_id=1, source_target_pairs={{0,4},{4,8},{8,12},{12,16},{16,20},{20,24},{24,28},{28,32},{32,36}... | collective-permute-start | bytes 8847368 | tf_op jit(solution)/shard_map/ppermute | solution.py:17
  271.6 1.3 copy-start.15
  273.0 251.2 %copy-start.9 = (f32[1,256,1,320]{1,3,0,2:T(8,128)S(1)}, f32[1,256,1,320]{1,3,0,2:T(8,128)}, u32[]{:S(2)}) copy-start(f32[1,256,1,320]{1,3,0,2:T(8,128)} %copy.110) | copy-start | bytes 983044
  519.8 4.4 copy-start.3
  524.1 2.1 copy-start.1
  (2 other events, 2.0 us)
where the time goes:
time: 534 us; the launch traced here: 526 us
  blocking collectives  272 us (51%)
  waiting for transfers between devices  97.7 us (18%)
  matrix products  54.3 us (10%)
  starting transfers between devices  45.8 us (9%)
  other arithmetic  28 us (5%)
  local copies, waits for them, and re-layouts  27.3 us (5%)
    psum x1, blocking collectives, on_device(): lax.psum((first_w, first_b, second_w, second_b), 'space')  241 us
    all_to_all x1, waiting for transfers between devices, on_device(): lax.all_to_all(masked, 'space', split_axis=3, concat_axis=2, tiled=True)  37.4 us
    ppermute x4, waiting for transfers between devices, with_halo(): lax.ppermute(head, axis, [((i + 1) % count, i) for i in range(ends)])  36 us
    psum x1, blocking collectives, on_device(): comb_total, back_total = lax.psum((comb_part, back_part), 'coil')  31 us
    dot_general x18, matrix products, kernel_grad(): jnp.einsum('ozxy,izxy->oi', cot_array, window, preferred_element_type=jnp...  25.6 us
    all_to_all x1, waiting for transfers between devices, on_device(): lax.all_to_all(cotangent, 'space', split_axis=3, concat_axis=2, tiled=True)  24.3 us
    conv_general_dilated x4, matrix products, plane_conv(): lax.conv_general_dilated(padded, kernel, (1, 1), ((0, 0), (1, 1)), dimens...  22.9 us
    ppermute x4, starting transfers between devices, with_halo(): lax.ppermute(tail, axis, [(i, (i + 1) % count) for i in range(ends)])  13.7 us
  transfers between devices with their start and end apart: 10, of which 3 were waited for; matrix products, arithmetic and copies ran while one was open for 11% of the time, Pallas kernels for 0%

commit v1 on v0

v1 whole, which is shorter than its diff:
```python
import math

import jax
import jax.numpy as jnp
import numpy as np
import ml_dtypes
from jax import lax
from jax.experimental import pallas as pl
from jax.experimental.pallas import tpu as pltpu
from jax.sharding import PartitionSpec as P

MESH = pl.DeviceIdType.MESH
BF = jnp.bfloat16
F32 = jnp.float32
NS, NCOIL = 64, 4
NY, NZ, CH, LINES = 320, 256, 18, 40
CL, ZL = 4, 4
BLK, NB = 32, 5
HV, HU, US = 34, 36, 40
MR, KR = 640, 256
PR = 176
TR = 192
LN = NB * 128


def one_hot(rows, cols, pairs):
    table = np.zeros((rows, cols), np.float32)
    for r, c in pairs:
        table[r, c] = 1.0
    return table


def dft_matrix(length):
    position = np.arange(length)
    angles = 2.0 * math.pi / length * ((position[:, None] * position[None, :]) % length)
    cosine = np.cos(angles) / math.sqrt(length)
    sine = np.sin(angles) / math.sqrt(length)
    return np.block([[cosine, sine], [-sine, cosine]]).astype(ml_dtypes.bfloat16)


def make_constants():
    bf = ml_dtypes.bfloat16
    hid = [(ch * HV + v, ch, v) for ch in range(CH) for v in range(HV)]
    inp = [((i * 3 + a) * US + u, i, a, u) for i in range(2) for a in range(3) for u in range(HU)]
    spread = one_hot(MR, 128, [(r, ch) for r, ch, _ in hid])
    pick1 = np.stack(
        [one_hot(128, KR, [(i * 9 + a * 3 + b, r) for r, i, a, _ in inp]) for b in range(3)]
    )
    pick2 = np.stack(
        [
            one_hot(128, KR, [(i * 9 + (2 - a) * 3 + (2 - b), r) for r, i, a, _ in inp])
            for b in range(3)
        ]
    )
    rowpick = np.stack(
        [
            one_hot(
                64, 128, [(q * BLK + t, q * 9 + a * 3 + b) for q in range(2) for t in range(BLK)]
            )
            for a in range(3)
            for b in range(3)
        ]
    )
    gap1 = np.full((MR, KR), 99.0, np.float32)
    for r, _, v in hid:
        for s, _, _, u in inp:
            gap1[r, s] = u - v
    gap2 = np.full((64, MR), 99.0, np.float32)
    for q in range(2):
        for t in range(BLK):
            for r, _, v in hid:
                gap2[q * BLK + t, r] = v - t
    inner = np.zeros((MR,), bool)
    for r, _, v in hid:
        inner[r] = 1 <= v <= BLK
    gap3 = np.where(inner[None, :], gap1.T, 99.0).astype(np.float32)
    sel_a = spread
    sel_b = np.roll(spread, 32, axis=1)
    middle = np.broadcast_to(inner[None, :], (8, MR)).astype(np.float32)
    edge = np.zeros((MR, 128), np.float32)
    for r, _, v in hid:
        edge[r] = 1.0 if v == 0 else 2.0 if v == HV - 1 else 0.0
    return [
        dft_matrix(NY),
        dft_matrix(NZ),
        spread.astype(bf),
        np.ascontiguousarray(spread.T).astype(bf),
        pick1.astype(bf),
        pick2.astype(bf),
        rowpick.astype(bf),
        gap1,
        gap2,
        gap3,
        sel_a,
        sel_b,
        middle,
        edge,
    ]


def mm(a, b):
    return jnp.dot(a, b, preferred_element_type=F32)


def mm_nt(a, b):
    return lax.dot_general(a, b, (((1,), (1,)), ((), ())), preferred_element_type=F32)


def cascade_kernel(*refs):
    n_const = 14
    k_hbm, cot_hbm, sens_hbm, lines_ref, lines2_ref, w1m_ref, w2m_ref, b1_ref, b2_ref = refs[:9]
    const_hbm = refs[9 : 9 + n_const]
    out_ref, gw_ref = refs[9 + n_const : 11 + n_const]
    rest = refs[11 + n_const :]
    consts = rest[:n_const]
    (
        kv, cv, sv, ksc, ksend, krecv, csc, csend, crecv, pos, ex, hsc, ht,
        img, part, rsrecv, hrecv, tmp, vbuf, hid, act, gp, bcol,
        w1b, w2f, w2b, w1f, agsend, agrecv, rows_a, rows_b, ar1, ar2, ar3,
        ld_sem, c_ld, k_s, k_r, c_s, c_r, rs_s, rs_r, h_s, h_r, ag_s, ag_r, ar_s, ar_r,
    ) = rest[n_const:]
    (ty, tz, spread, spread_t, pick1, pick2, rowpick, gap1, gap2, gap3, sel_a, sel_b, middle, edge) = consts

    me = lax.axis_index("space")
    co = lax.axis_index("coil")
    hz = co // 2
    hy = co % 2

    barrier = pltpu.get_barrier_semaphore()

    def greet(j, _):
        pl.semaphore_signal(
            barrier, inc=1, device_id=(lax.rem(me + j, NS), co), device_id_type=MESH
        )
        return 0

    lax.fori_loop(1, NS, greet, 0)
    for j in range(1, NCOIL):
        pl.semaphore_signal(
            barrier, inc=1, device_id=(me, lax.rem(co + j, NCOIL)), device_id_type=MESH
        )
    load_k = pltpu.make_async_copy(k_hbm, kv, ld_sem.at[0])
    load_c = pltpu.make_async_copy(cot_hbm, cv, ld_sem.at[1])
    load_s = pltpu.make_async_copy(sens_hbm, sv, ld_sem.at[2])
    load_k.start()
    load_c.start()
    loads = [
        pltpu.make_async_copy(src, dst, c_ld.at[n])
        for n, (src, dst) in enumerate(zip(const_hbm, consts))
    ]
    for load in loads:
        load.start()
    load_s.start()

    load_k.wait()
    y_rows = lax.broadcasted_iota(jnp.int32, (NY, 128), 0)

    def hot(z):
        row = lines2_ref[pl.ds(me * ZL + z, 1), :]
        return jnp.where(y_rows == row, 1.0, 0.0).astype(BF)

    hots = [hot(z) for z in range(ZL)]
    for p in range(2):
        for zlo in range(2):
            packed = mm(kv[p, :, zlo].reshape(CL * NS, NY), hots[zlo])
            packed += mm(kv[p, :, zlo + 2].reshape(CL * NS, NY), hots[zlo + 2])
            ksc[pl.ds((p * 2 + zlo) * 256, 256), :] = packed

    def pack_k(x, _):
        ksend[x] = ksc[pl.ds(x, 16, stride=NS), :].astype(BF)
        return 0

    lax.fori_loop(0, NS, pack_k, 0, unroll=4)

    pl.semaphore_wait(barrier, NS - 1 + NCOIL - 1)

    def spread_out(src, dst, s_sem, r_sem):
        pltpu.make_async_copy(src.at[me], dst.at[me], r_sem).start()

        def send(j, _):
            to = lax.rem(me + j, NS)
            pltpu.make_async_remote_copy(
                src_ref=src.at[to],
                dst_ref=dst.at[me],
                send_sem=s_sem,
                recv_sem=r_sem,
                device_id=(to, co),
                device_id_type=MESH,
            ).start()
            return 0

        lax.fori_loop(1, NS, send, 0)

    spread_out(ksend, krecv, k_s, k_r)

    load_c.wait()
    loads[0].wait()

    def cot_y(zl, _):
        rows = mm(cv[0, :, zl].reshape(CL * NS, NY), ty[0:NY])
        rows += mm(cv[1, :, zl].reshape(CL * NS, NY), ty[NY:])
        for j in range(5):
            csc[j, pl.ds(pl.multiple_of(zl * 256, 256), 256), :] = rows[:, j * 128 : (j + 1) * 128]
        return 0

    lax.fori_loop(0, ZL, cot_y, 0)

    def pack_c(x, _):
        for j in range(5):
            lanes = slice(j * 128, (j + 1) * 128)
            csend[x, :, lanes] = csc[j, pl.ds(x, 16, stride=NS), :].astype(BF)
        return 0

    lax.fori_loop(0, NS, pack_c, 0, unroll=2)
    spread_out(csend, crecv, c_s, c_r)

    for load in loads[1:]:
        load.wait()
    lane_y = lax.broadcasted_iota(jnp.int32, (32, MR), 1)
    lane_y = jnp.where(lane_y >= NY, lane_y - NY, lane_y)
    upper = jnp.where(lax.broadcasted_iota(jnp.int32, (32, MR), 0) % 4 >= 2, 64, 0)

    def find(g, _):
        rows = pl.ds(pl.multiple_of(g * 32, 32), 32)
        lines = lines_ref[rows, :]
        place = jnp.full((32, MR), 127, jnp.int32)
        for line in range(LINES):
            place = jnp.where(lines[:, line : line + 1] == lane_y, upper + line, place)
        pos[rows, :] = place
        return 0

    lax.fori_loop(0, NZ // 32, find, 0)

    w1 = w1m_ref[...]
    w2 = w2m_ref[...]
    sp = spread[...]
    spt = spread_t[...]
    by_hidden1 = mm(sp, w1).astype(BF)
    by_hidden2 = mm(sp, w2).astype(BF)
    band1 = jnp.zeros((MR, KR), F32)
    band2 = jnp.zeros((MR, KR), F32)
    for b in range(3):
        hit = gap1[...] == float(b)
        band1 += jnp.where(hit, mm(by_hidden1, pick1[b]), 0.0)
        band2 += jnp.where(hit, mm(by_hidden2, pick2[b]), 0.0)
    w1b[...] = band1.astype(BF)
    w2f[...] = band2.astype(BF)
    for a in range(3):
        out2 = jnp.zeros((64, MR), F32)
        out1 = jnp.zeros((64, MR), F32)
        for b in range(3):
            hit = gap2[...] == float(b)
            out2 += jnp.where(hit, mm(mm_nt(rowpick[a * 3 + b], w2).astype(BF), spt), 0.0)
            flipped = rowpick[(2 - a) * 3 + (2 - b)]
            out1 += jnp.where(hit, mm(mm_nt(flipped, w1).astype(BF), spt), 0.0)
        w2b[a] = out2.astype(BF)
        w1f[a] = out1.astype(BF)
    bias = jnp.sum(sp.astype(F32) * b1_ref[...], axis=1, keepdims=True)
    bcol[...] = jnp.broadcast_to(bias, (MR, 128))
    zero_rows = jnp.zeros((KR - 6 * US, 3 * LN), BF)
    for n in range(2):
        vbuf[n, 6 * US :, :] = zero_rows
    for j in range(5):
        for i in range(2):
            tmp[j, i, 0:8, :] = jnp.zeros((8, 128), F32)
            tmp[j, i, 176:TR, :] = jnp.zeros((TR - 176, 128), F32)
    load_s.wait()

    def to_image(n):
        def one_coil(c, _):
            for j in range(5):
                block = hsc[j, pl.ds(c, NZ, stride=CL), :]
                ht[j * 128 : (j + 1) * 128, :] = block.T.astype(BF)
            both = jnp.concatenate([ht[0:NY, :], ht[NY:, :]], axis=1)
            img[n, c] = mm(both, tz[...]).astype(BF)
            return 0

        lax.fori_loop(0, CL, one_coil, 0)

        def combine(g, _):
            rows = pl.ds(pl.multiple_of(g * 16, 16), 16)
            re = jnp.zeros((16, NZ), F32)
            im = jnp.zeros((16, NZ), F32)
            for c in range(CL):
                both = img[n, c, rows, :].astype(F32)
                i0, i1 = both[:, :NZ], both[:, NZ:]
                s0 = sv[0, c, rows, :].astype(F32)
                s1 = sv[1, c, rows, :].astype(F32)
                re += s0 * i0 + s1 * i1
                im += s0 * i1 - s1 * i0
            if n == 1:
                re, im = -re, -im
            part[n, 0, rows, :] = re.astype(BF)
            part[n, 1, rows, :] = im.astype(BF)
            return 0

        lax.fori_loop(0, NY // 16, combine, 0)

    def piece(n, to):
        return part.at[
            n,
            :,
            pl.ds(pl.multiple_of((to % 2) * 144, 16), PR),
            pl.ds(pl.multiple_of((to // 2) * 128, 128), 128),
        ]

    def coil_send(n):
        pltpu.make_async_copy(piece(n, co), rsrecv.at[n, co], rs_r.at[n]).start()
        for j in range(1, NCOIL):
            to = lax.rem(co + j, NCOIL)
            pltpu.make_async_remote_copy(
                src_ref=piece(n, to),
                dst_ref=rsrecv.at[n, co],
                send_sem=rs_s.at[n],
                recv_sem=rs_r.at[n],
                device_id=(me, to),
                device_id_type=MESH,
            ).start()

    def coil_sum(n):
        pltpu.make_async_copy(rsrecv.at[n], rsrecv.at[n], rs_r.at[n]).wait()
        for q in range(2):
            total = rsrecv[n, 0, q].astype(F32)
            for j in range(1, NCOIL):
                total += rsrecv[n, j, q].astype(F32)
            hrecv[n, 4, q] = total.astype(BF)
        for slot, off in enumerate((-2, -1, 1, 2)):
            to = lax.rem(me + off + NS, NS)
            pltpu.make_async_remote_copy(
                src_ref=hrecv.at[n, 4],
                dst_ref=hrecv.at[n, 3 - slot],
                send_sem=h_s.at[n],
                recv_sem=h_r.at[n],
                device_id=(to, co),
                device_id_type=MESH,
            ).start()

    def windows(n):
        pltpu.make_async_copy(hrecv.at[n, pl.ds(0, 4)], hrecv.at[n, pl.ds(0, 4)], h_r.at[n]).wait()
        for j, slot in enumerate((0, 1, 4, 2, 3)):
            x = me + j - 2
            inside = jnp.logical_and(x >= 0, x < NS)
            for q in range(2):
                got = hrecv[n, slot, q].astype(F32)
                tmp[j, q, 2 : 2 + PR, :] = jnp.where(inside, got, 0.0)
        for x3 in range(3):
            for blk in range(NB):
                lanes = slice((x3 * NB + blk) * 128, (x3 * NB + blk + 1) * 128)
                rows = pl.ds(pl.multiple_of(hy * 16, 16) + blk * BLK, US)
                column = [tmp[x3 + a, q, rows, :] for q in range(2) for a in range(3)]
                vbuf[n, 0 : 6 * US, lanes] = jnp.concatenate(column, axis=0).astype(BF)

    def into_hidden(n, w):
        for x3 in range(3):
            lanes = slice(x3 * LN, (x3 + 1) * LN)
            hid[n, :, lanes] = mm(w[...], vbuf[n, :, lanes])

    x_ok = [jnp.logical_and(me + d >= 0, me + d < NS) for d in (-1, 0, 1)]

    def keep(value, kind, x3, blk):
        if blk == 0:
            value = jnp.where(jnp.logical_and(kind == 1.0, hy == 0), 0.0, value)
        if blk == NB - 1:
            value = jnp.where(jnp.logical_and(kind == 2.0, hy == 1), 0.0, value)
        if x3 != 1:
            value = jnp.where(x_ok[x3], value, 0.0)
        return value

    def out_of_hidden(values, w):
        total = mm(w[0], values[:, 0:LN])
        total += mm(w[1], values[:, LN : 2 * LN])
        total += mm(w[2], values[:, 2 * LN :])
        return total

    def gather_send(n):
        pltpu.make_async_copy(agsend.at[n], agrecv.at[n, co], ag_r.at[n]).start()
        for j in range(1, NCOIL):
            to = lax.rem(co + j, NCOIL)
            pltpu.make_async_remote_copy(
                src_ref=agsend.at[n],
                dst_ref=agrecv.at[n, co],
                send_sem=ag_s.at[n],
                recv_sem=ag_r.at[n],
                device_id=(me, to),
                device_id_type=MESH,
            ).start()

    pltpu.make_async_copy(krecv, krecv, k_r).wait()
    low_rows = lax.broadcasted_iota(jnp.int32, (8, MR), 0) < 4
    low_lanes = lax.broadcasted_iota(jnp.int32, (8, 128), 1) < 64

    def pick(values, index):
        return jnp.take_along_axis(values, index, axis=1, mode="promise_in_bounds")

    def expand(s, _):
        got = krecv[s].astype(F32)
        halves = []
        for zhi in range(2):
            first = pos[pl.ds(s * 4 + 2 * zhi, 1), :]
            second = pos[pl.ds(s * 4 + 2 * zhi + 1, 1), :]
            index = jnp.where(
                low_rows,
                jnp.broadcast_to(first, (8, MR)),
                jnp.broadcast_to(second, (8, MR)),
            )
            at = [index[:, j * 128 : (j + 1) * 128] for j in range(5)]
            re, im = got[0:8], got[8:16]
            halves.append(
                jnp.concatenate(
                    [
                        pick(re, at[0]),
                        pick(re, at[1]),
                        jnp.where(low_lanes, pick(re, at[2]), pick(im, at[2])),
                        pick(im, at[3]),
                        pick(im, at[4]),
                    ],
                    axis=1,
                )
            )
        ex[pl.ds(pl.multiple_of(s * 16, 16), 16), :] = jnp.concatenate(halves, axis=0).astype(BF)
        return 0

    lax.fori_loop(0, NS, expand, 0, unroll=2)

    def k_y(g, _):
        rows = pl.ds(pl.multiple_of(g * 256, 256), 256)
        half = mm(ex[rows, :], ty[...]).astype(BF).astype(F32)
        for j in range(5):
            hsc[j, rows, :] = half[:, j * 128 : (j + 1) * 128]
        return 0

    lax.fori_loop(0, 4, k_y, 0)
    to_image(0)
    coil_send(0)
    coil_sum(0)
    windows(0)
    into_hidden(0, w1b)

    def activate(g, _):
        rows = pl.ds(pl.multiple_of(g * 16, 16), 16)
        kind = edge[rows, :]
        add = bcol[rows, :]
        for x3 in range(3):
            for blk in range(NB):
                lanes = slice((x3 * NB + blk) * 128, (x3 * NB + blk + 1) * 128)
                h = hid[0, rows, lanes] + add
                s = 0.5 * jnp.tanh(0.5 * h) + 0.5
                act[rows, lanes] = keep(h * s, kind, x3, blk).astype(BF)
                hid[0, rows, lanes] = s * (1.0 + h * (1.0 - s))
        return 0

    lax.fori_loop(0, MR // 16, activate, 0)
    regularized = out_of_hidden(act, w2b)
    for q in range(2):
        for blk in range(NB):
            block = regularized[q * BLK : (q + 1) * BLK, blk * 128 : (blk + 1) * 128] + b2_ref[q]
            agsend[0, q, blk * BLK : (blk + 1) * BLK, :] = block.astype(BF)
    gather_send(0)

    pltpu.make_async_copy(crecv, crecv, c_r).wait()

    def widen(s, _):
        got = crecv[s].astype(F32)
        for j in range(5):
            hsc[j, pl.ds(pl.multiple_of(s * 16, 16), 16), :] = got[:, j * 128 : (j + 1) * 128]
        return 0

    lax.fori_loop(0, NS, widen, 0, unroll=4)
    to_image(1)
    coil_send(1)
    coil_sum(1)
    windows(1)
    into_hidden(1, w2f)

    def grad_hidden(g, _):
        rows = pl.ds(pl.multiple_of(g * 16, 16), 16)
        kind = edge[rows, :]
        for x3 in range(3):
            for blk in range(NB):
                lanes = slice((x3 * NB + blk) * 128, (x3 * NB + blk + 1) * 128)
                value = hid[1, rows, lanes] * hid[0, rows, lanes]
                gp[rows, lanes] = keep(value, kind, x3, blk).astype(BF)
        return 0

    lax.fori_loop(0, MR // 16, grad_hidden, 0)
    grad_comb = out_of_hidden(gp, w1f)
    for q in range(2):
        for blk in range(NB):
            block = grad_comb[q * BLK : (q + 1) * BLK, blk * 128 : (blk + 1) * 128]
            agsend[1, q, blk * BLK : (blk + 1) * BLK, :] = block.astype(BF)
    gather_send(1)

    rows_a[...] = jnp.zeros((24, MR), F32)
    rows_b[...] = jnp.zeros((24, MR), F32)
    gp_mid = gp[:, LN : 2 * LN]
    cross = mm_nt(vbuf[0, :, LN : 2 * LN], gp_mid)
    for i in range(2):
        for a in range(3):
            rows = slice((i * 3 + a) * US, (i * 3 + a + 1) * US)
            block = cross[rows, :]
            gap = gap3[rows, :]
            for b in range(3):
                at = i * 9 + a * 3 + b
                rows_a[at : at + 1, :] = jnp.sum(
                    jnp.where(gap == float(b), block, 0.0), axis=0, keepdims=True
                )
    sums = mm_nt(jnp.ones((8, LN), BF), gp_mid) * middle[...]
    rows_a[18:19, :] = sums[0:1, :]
    own = jnp.concatenate(
        [
            jnp.concatenate(
                [
                    hrecv[1, 4, q, pl.ds(pl.multiple_of(hy * 16, 16) + blk * BLK, BLK), :]
                    for blk in range(NB)
                ],
                axis=1,
            )
            for q in range(2)
        ],
        axis=0,
    )
    for a in range(3):
        cross = mm_nt(own, act[:, a * LN : (a + 1) * LN])
        for q in range(2):
            rows = slice(q * BLK, (q + 1) * BLK)
            for b in range(3):
                at = a * 6 + b * 2 + q
                rows_b[at : at + 1, :] = jnp.sum(
                    jnp.where(gap2[rows, :] == float(b), cross[rows, :], 0.0),
                    axis=0,
                    keepdims=True,
                )
    high = lax.Precision.HIGHEST
    grads = jnp.dot(rows_a[...], sel_a[...], precision=high, preferred_element_type=F32)
    grads += jnp.dot(rows_b[...], sel_b[...], precision=high, preferred_element_type=F32)
    at_row = lax.broadcasted_iota(jnp.int32, (24, 128), 0)
    at_lane = lax.broadcasted_iota(jnp.int32, (24, 128), 1)
    own_f = own.astype(F32)
    for q in range(2):
        spot = jnp.logical_and(at_row == 18, at_lane == 32 + q)
        grads += jnp.where(spot, jnp.sum(own_f[q * BLK : (q + 1) * BLK]), 0.0)

    def share(n, buf, count, mine, device):
        buf[mine] = grads_in[n]
        for j in range(1, count):
            to = lax.rem(mine + j, count)
            pltpu.make_async_remote_copy(
                src_ref=buf.at[mine],
                dst_ref=buf.at[mine],
                send_sem=ar_s.at[n],
                recv_sem=ar_r.at[n],
                device_id=device(to),
                device_id_type=MESH,
            ).start()

    def collect(n, buf, count):
        rest_of = buf.at[pl.ds(0, count - 1)]
        pltpu.make_async_copy(rest_of, rest_of, ar_r.at[n]).wait()
        total = buf[0]
        for j in range(1, count):
            total += buf[j]
        return total

    row_y, row_zc = me // 16, me % 16
    grads_in = [grads]
    share(0, ar1, 16, row_zc, lambda to: (row_y * 16 + to, co))

    pltpu.make_async_copy(agrecv.at[0], agrecv.at[0], ag_r.at[0]).wait()
    pltpu.make_async_copy(agrecv.at[1], agrecv.at[1], ag_r.at[1]).wait()

    def finish(g, _):
        for half_y in range(2):
            for half_z in range(2):
                slot = half_z * 2 + half_y
                src = pl.ds(pl.multiple_of(g * 16, 16), 16)
                dst = pl.ds(pl.multiple_of(half_y * 160 + g * 16, 16), 16)
                lo = slice(half_z * 128, half_z * 128 + 128)
                hi = slice(NZ + half_z * 128, NZ + half_z * 128 + 128)
                r0 = agrecv[0, slot, 0, src, :].astype(F32)
                r1 = agrecv[0, slot, 1, src, :].astype(F32)
                g0 = agrecv[1, slot, 0, src, :].astype(F32)
                g1 = agrecv[1, slot, 1, src, :].astype(F32)
                for c in range(CL):
                    i0 = img[0, c, dst, lo].astype(F32)
                    i1 = img[0, c, dst, hi].astype(F32)
                    k0 = img[1, c, dst, lo].astype(F32)
                    k1 = img[1, c, dst, hi].astype(F32)
                    re = -(k0 * r0 + k1 * r1) + i0 * g0 + i1 * g1
                    im = -(k1 * r0 - k0 * r1) + i1 * g0 - i0 * g1
                    out_ref[0, c, dst, lo] = re.astype(BF)
                    out_ref[1, c, dst, lo] = im.astype(BF)
        return 0

    lax.fori_loop(0, 10, finish, 0)

    grads_in.append(collect(0, ar1, 16))
    share(1, ar2, 4, row_y, lambda to: (to * 16 + row_zc, co))
    grads_in.append(collect(1, ar2, 4))
    share(2, ar3, 4, co, lambda to: (me, to))
    gw_ref[...] = collect(2, ar3, 4) * (1.0 / math.sqrt(NS * NY * NZ))

    def sent(ref, sem):
        pltpu.make_async_copy(ref, ref, sem).wait()

    sent(ksend.at[pl.ds(0, NS - 1)], k_s)
    sent(csend.at[pl.ds(0, NS - 1)], c_s)
    for n in range(2):
        sent(rsrecv.at[n, pl.ds(0, NCOIL - 1)], rs_s.at[n])
        sent(hrecv.at[n, pl.ds(0, 4)], h_s.at[n])
        sent(agrecv.at[n, pl.ds(0, NCOIL - 1)], ag_s.at[n])
    sent(ar1.at[pl.ds(0, 15)], ar_s.at[0])
    sent(ar2.at[pl.ds(0, 3)], ar_s.at[1])
    sent(ar3.at[pl.ds(0, 3)], ar_s.at[2])


def on_device(k_space, cotangent, sens_maps, line_index, w_first, b_first, w_second, b_second):
    constants = make_constants()
    sens = jnp.transpose(sens_maps.reshape(2, CL, NZ, NY), (0, 1, 3, 2))
    lines = jnp.pad(line_index, ((0, 0), (0, 128 - LINES)), constant_values=-1)
    upper = (jnp.arange(NZ) % 4 >= 2)[:, None]
    lines2 = jnp.where(upper, jnp.roll(lines, 64, axis=1), lines)
    w1m = jnp.pad(w_first.reshape(CH, 18), ((0, 128 - CH), (0, 110)))
    w2m = jnp.pad(jnp.transpose(w_second, (1, 0, 2, 3)).reshape(CH, 18), ((0, 128 - CH), (0, 110)))
    b1 = jnp.pad(b_first, (0, 110)).reshape(1, 128)
    vm = pl.BlockSpec(memory_space=pltpu.VMEM)
    anym = pl.BlockSpec(memory_space=pl.ANY)
    dma = pltpu.SemaphoreType.DMA
    scratch = [pltpu.VMEM(c.shape, c.dtype) for c in constants]
    scratch += [
        pltpu.VMEM((2, CL, ZL, NS, NY), BF),
        pltpu.VMEM((2, CL, ZL, NS, NY), BF),
        pltpu.VMEM((2, CL, NY, NZ), BF),
        pltpu.VMEM((16 * NS, 128), F32),
        pltpu.VMEM((NS, 16, 128), BF),
        pltpu.VMEM((NS, 16, 128), BF),
        pltpu.VMEM((5, 16 * NS, 128), F32),
        pltpu.VMEM((NS, 16, 640), BF),
        pltpu.VMEM((NS, 16, 640), BF),
        pltpu.VMEM((NZ, 640), jnp.int32),
        pltpu.VMEM((NZ * CL, 640), BF),
        pltpu.VMEM((5, NZ * CL, 128), F32),
        pltpu.VMEM((640, NZ), BF),
        pltpu.VMEM((2, CL, NY, 2 * NZ), BF),
        pltpu.VMEM((2, 2, NY, NZ), BF),
        pltpu.VMEM((2, NCOIL, 2, PR, 128), BF),
        pltpu.VMEM((2, 5, 2, PR, 128), BF),
        pltpu.VMEM((5, 2, TR, 128), F32),
        pltpu.VMEM((2, KR, 3 * LN), BF),
        pltpu.VMEM((2, MR, 3 * LN), F32),
        pltpu.VMEM((MR, 3 * LN), BF),
        pltpu.VMEM((MR, 3 * LN), BF),
        pltpu.VMEM((MR, 128), F32),
        pltpu.VMEM((MR, KR), BF),
        pltpu.VMEM((MR, KR), BF),
        pltpu.VMEM((3, 64, MR), BF),
        pltpu.VMEM((3, 64, MR), BF),
        pltpu.VMEM((2, 2, NY // 2, 128), BF),
        pltpu.VMEM((2, NCOIL, 2, NY // 2, 128), BF),
        pltpu.VMEM((24, MR), F32),
        pltpu.VMEM((24, MR), F32),
        pltpu.VMEM((16, 24, 128), F32),
        pltpu.VMEM((4, 24, 128), F32),
        pltpu.VMEM((4, 24, 128), F32),
        dma((3,)),
        dma((len(constants),)),
        dma,
        dma,
        dma,
        dma,
        dma((2,)),
        dma((2,)),
        dma((2,)),
        dma((2,)),
        dma((2,)),
        dma((2,)),
        dma((3,)),
        dma((3,)),
    ]
    grad_sens, grads = pl.pallas_call(
        cascade_kernel,
        out_shape=(
            jax.ShapeDtypeStruct((2, CL, NY, NZ), BF),
            jax.ShapeDtypeStruct((24, 128), F32),
        ),
        in_specs=[anym] * 3
        + [vm] * 5
        + [pl.BlockSpec(memory_space=pltpu.SMEM)]
        + [anym] * len(constants),
        out_specs=(vm, vm),
        scratch_shapes=scratch,
        compiler_params=pltpu.CompilerParams(
            collective_id=0, has_side_effects=True, vmem_limit_bytes=60 * 1024 * 1024
        ),
    )(k_space, cotangent, sens, lines, lines2, w1m, w2m, b1, b_second, *constants)
    grad_sens = jnp.transpose(grad_sens, (0, 1, 3, 2)).reshape(2, CL, NZ, 1, NY)
    grad_w1 = jnp.transpose(grads[0:18, 0:CH]).reshape(CH, 2, 3, 3)
    grad_b1 = grads[18, 0:CH]
    grad_w2 = jnp.transpose(grads[0:18, 32 : 32 + CH].reshape(3, 3, 2, CH), (2, 3, 0, 1))
    grad_b2 = grads[18, 32:34]
    return (grad_sens, grad_w1, grad_b1, grad_w2, grad_b2)


def solution(mesh):
    placed = (
        P(None, "coil", "space", None, None),
        P(None, "coil", "space", None, None),
        P(None, "coil", None, "space", None),
        P(),
        P(),
        P(),
        P(),
        P(),
    )
    return jax.shard_map(
        on_device,
        mesh=mesh,
        in_specs=placed,
        out_specs=(P(None, "coil", None, "space", None), P(), P(), P(), P()),
        check_vma=False,
    )
```

time: 534 us -> 105 us (0.20); the launches traced: 526 us -> 103 us
  blocking collectives: 272 us -> 0 us
  waiting for transfers between devices: 97.7 us -> 0 us
  Pallas kernels: 0 us -> 90 us
  matrix products: 54.3 us -> 0 us
  starting transfers between devices: 45.8 us -> 0 us
  other arithmetic: 28 us -> 0.8 us
  local copies, waits for them, and re-layouts: 27.3 us -> 11.9 us
    psum x2 -> x0, blocking collectives: 272 us -> none  [the longest x1 241 us: on_device(): lax.psum((first_w, first_b, second_w, second_b), 'space')]
    pallas_call x0 -> x1, Pallas kernels: none -> 90 us  [on_device(): pl.pallas_call(cascade_kernel, out_shape=(jax.ShapeDtypeStruct((2, CL, NY...]
    all_to_all x2 -> x0, waiting for transfers between devices: 61.7 us -> none  [the longest x1 37.4 us: on_device(): lax.all_to_all(masked, 'space', split_axis=3, concat_axis=2, tiled=True)]
    ppermute x8 -> x0, waiting for transfers between devices: 36 us -> none  [the longest x4 36 us: with_halo(): lax.ppermute(head, axis, [((i + 1) % count, i) for i in range(ends)])]
    dot_general x22 -> x0, matrix products: 31.4 us -> none  [the longest x18 25.6 us: kernel_grad(): jnp.einsum('ozxy,izxy->oi', cot_array, window, preferred_element_type=jnp...]
    ppermute x8 -> x0, starting transfers between devices: 26.1 us -> none  [the longest x4 13.7 us: with_halo(): lax.ppermute(tail, axis, [(i, (i + 1) % count) for i in range(ends)])]
    conv_general_dilated x4 -> x0, matrix products: 22.9 us -> none  [plane_conv(): lax.conv_general_dilated(padded, kernel, (1, 1), ((0, 0), (1, 1)), dimens...]
    all_to_all x2 -> x0, starting transfers between devices: 19.7 us -> none  [the longest x1 13.2 us: on_device(): lax.all_to_all(masked, 'space', split_axis=3, concat_axis=2, tiled=True)]
  transfers between devices with their start and end apart: 10 -> 0, of which waited for: 3 -> 0; matrix products, arithmetic and copies ran while one was open for 11% -> 0% of each run, Pallas kernels for 0% -> 0%
where the time goes in v1:
time: 105 us; the launch traced here: 103 us
  Pallas kernels  90 us (86%)
  local copies, waits for them, and re-layouts  11.9 us (11%)
    pallas_call x1, Pallas kernels, on_device(): pl.pallas_call(cascade_kernel, out_shape=(jax.ShapeDtypeStruct((2, CL, NY...  90 us
    unnamed x4, local copies, waits for them, and re-layouts  4.62 us

profile of v1, /device:TPU:1, one launch (start us, length us, event | category | flops | bytes accessed | tf_op | source)
XLA Modules:
  0.0 103.4 jit_solution(12111061418206850778)
XLA Ops:
  0.6 1.2 %pad_bitcast_fusion.refs_7_ = f32[1,128]{1,0:T(1,128)} fusion(f32[18]{0:T(128)} %param.27), kind=kLoop, calls=%fused_computation.6 | loop fusion | bytes 584 | tf_op jit(solution)/shard_map/reshape | solution.py:624
  1.8 0.7 copy.33
  2.5 0.1 copy.34
  2.6 0.7 copy.35
  3.3 0.1 copy.36
  3.4 0.6 pad.18.refs_6_
  4.1 0.6 pad.17.refs_5_
  4.7 0.9 copy.32
  5.6 0.8 pad_select_fusion
  6.4 90.0 %shard_map.245 = (bf16[2,4,320,256]{3,2,1,0:T(8,128)(2,1)}, f32[24,128]{1,0:T(8,128)}) custom-call(bf16[2,4,4,64,320]{4,3,2,1,0:T(8,128)(2,1)} %refs_0_.1, bf16[2,4,4,64,320]{4,3,2,1,0:T(8,128)(2,1)} %refs_1_.1, bf16[2,4,320,256]{3,2,1,0:T(8,128)(2,1)} %bitcast.24, s32[256,128]{1,0:T(8,128)} %get-tuple-element.20.refs_3_, ...), custom_call_target="tpu_custom_call" | custom-call | tf_op jit(solution)/shard_map/pallas_call | solution.py:679
  96.4 1.2 %slice_bitcast_fusion.2 = f32[18]{0:T(128)} fusion(f32[24,128]{1,0:T(8,128)} %get-tuple-element.8), kind=kLoop, calls=%fused_computation.5 | loop fusion | bytes 144 | tf_op jit(solution)/shard_map/squeeze | solution.py:697
  97.6 1.3 %slice_bitcast_fusion.1 = f32[2]{0:T(128)} fusion(f32[24,128]{1,0:T(8,128)} %get-tuple-element.8), kind=kLoop, calls=%fused_computation.4 | loop fusion | bytes 16 | tf_op jit(solution)/shard_map/squeeze | solution.py:699
  98.9 0.9 fusion.1
  99.7 0.6 reshape.47
  100.3 0.6 copy.38
  100.9 2.5 %copy.40 = bf16[2,4,256,1,320]{2,4,3,1,0:T(8,128)(2,1)} copy(bf16[2,4,256,1,320]{2,4,3,1,0:T(8,128)(2,1)} %bitcast.25) | data formatting | bytes 2621440
  (5 shorter events, 0.1 us)

commit v2 on v1

--- a/solution.py
+++ b/solution.py
@@ -21,6 +21,18 @@
 PR = 176
 TR = 192
 LN = NB * 128
+NCH = 5
+GROUPS = ((0, 2), (2, 4), (4, 5))
+PIECES = (
+    (0, 0, 0, 64, 0),
+    (1, 0, 64, 48, 0),
+    (1, 0, 112, 16, 1),
+    (2, 0, 128, 48, 1),
+    (2, 1, 144, 48, 0),
+    (3, 1, 192, 64, 0),
+    (4, 1, 256, 64, 1),
+)
+STEPS = ((0, 112), (112, 64))
 
 
 def one_hot(rows, cols, pairs):
@@ -40,22 +52,24 @@
 
 def make_constants():
     bf = ml_dtypes.bfloat16
+    table_y = dft_matrix(NY).reshape(2 * NY, 2, NCH, 64)
+    table_y = np.ascontiguousarray(table_y.transpose(0, 2, 1, 3)).reshape(2 * NY, 2 * NY)
     hid = [(ch * HV + v, ch, v) for ch in range(CH) for v in range(HV)]
     inp = [((i * 3 + a) * US + u, i, a, u) for i in range(2) for a in range(3) for u in range(HU)]
     spread = one_hot(MR, 128, [(r, ch) for r, ch, _ in hid])
     pick1 = np.stack(
-        [one_hot(128, KR, [(i * 9 + a * 3 + b, r) for r, i, a, _ in inp]) for b in range(3)]
+        [one_hot(128, KR, [((a * 3 + b) * 2 + i, r) for r, i, a, _ in inp]) for b in range(3)]
     )
     pick2 = np.stack(
         [
-            one_hot(128, KR, [(i * 9 + (2 - a) * 3 + (2 - b), r) for r, i, a, _ in inp])
+            one_hot(128, KR, [((8 - a * 3 - b) * 2 + i, r) for r, i, a, _ in inp])
             for b in range(3)
         ]
     )
     rowpick = np.stack(
         [
             one_hot(
-                64, 128, [(q * BLK + t, q * 9 + a * 3 + b) for q in range(2) for t in range(BLK)]
+                64, 128, [(q * BLK + t, (a * 3 + b) * 2 + q) for q in range(2) for t in range(BLK)]
             )
             for a in range(3)
             for b in range(3)
@@ -81,7 +95,7 @@
     for r, _, v in hid:
         edge[r] = 1.0 if v == 0 else 2.0 if v == HV - 1 else 0.0
     return [
-        dft_matrix(NY),
+        table_y,
         dft_matrix(NZ),
         spread.astype(bf),
         np.ascontiguousarray(spread.T).astype(bf),
@@ -106,21 +120,26 @@
     return lax.dot_general(a, b, (((1,), (1,)), ((), ())), preferred_element_type=F32)
 
 
+def arrived(ref, sem):
+    pltpu.make_async_copy(ref, ref, sem).wait()
+
+
 def cascade_kernel(*refs):
     n_const = 14
-    k_hbm, cot_hbm, sens_hbm, lines_ref, lines2_ref, w1m_ref, w2m_ref, b1_ref, b2_ref = refs[:9]
-    const_hbm = refs[9 : 9 + n_const]
-    out_ref, gw_ref = refs[9 + n_const : 11 + n_const]
-    rest = refs[11 + n_const :]
+    k_hbm, cot_hbm, sens_hbm, index_ref, first_ref, second_ref, b1_ref, b2_ref = refs[:8]
+    const_hbm = refs[8 : 8 + n_const]
+    pre_hbm, gw_ref = refs[8 + n_const : 10 + n_const]
+    rest = refs[10 + n_const :]
     consts = rest[:n_const]
     (
-        kv, cv, sv, ksc, ksend, krecv, csc, csend, crecv, pos, ex, hsc, ht,
+        kv, cv, sv, ksc, ksend, krecv, csc, cs0, cs1, cs2, cr0, cr1, cr2, pos, ex, hsc,
         img, part, rsrecv, hrecv, tmp, vbuf, hid, act, gp, bcol,
-        w1b, w2f, w2b, w1f, agsend, agrecv, rows_a, rows_b, ar1, ar2, ar3,
-        ld_sem, c_ld, k_s, k_r, c_s, c_r, rs_s, rs_r, h_s, h_r, ag_s, ag_r, ar_s, ar_r,
+        w1b, w2f, w2b, w1f, agsend, agrecv, regpart, outv, rows_a, rows_b, gsec, ar1, ar2, lines_ref, lines2_ref, wt,
+        ld_sem, c_ld, o_sem, k_s, k_r, c_s, c_r, rs_s, rs_r, h_s, h_r, ag_s, ag_r, ar_s, ar_r,
     ) = rest[n_const:]
     (ty, tz, spread, spread_t, pick1, pick2, rowpick, gap1, gap2, gap3, sel_a, sel_b, middle, edge) = consts
 
+    csend, crecv = (cs0, cs1, cs2), (cr0, cr1, cr2)
     me = lax.axis_index("space")
     co = lax.axis_index("coil")
     hz = co // 2
@@ -139,6 +158,11 @@
         pl.semaphore_signal(
             barrier, inc=1, device_id=(me, lax.rem(co + j, NCOIL)), device_id_type=MESH
         )
+    row_y, row_zc = me // 16, me % 16
+    for jy in range(1, 4):
+        for jc in range(1, NCOIL):
+            there = (lax.rem(row_y + jy, 4) * 16 + row_zc, lax.rem(co + jc, NCOIL))
+            pl.semaphore_signal(barrier, inc=1, device_id=there, device_id_type=MESH)
     load_k = pltpu.make_async_copy(k_hbm, kv, ld_sem.at[0])
     load_c = pltpu.make_async_copy(cot_hbm, cv, ld_sem.at[1])
     load_s = pltpu.make_async_copy(sens_hbm, sv, ld_sem.at[2])
@@ -152,6 +176,15 @@
         load.start()
     load_s.start()
 
+    turned = jnp.concatenate(
+        [index_ref[...].astype(F32), jnp.full((128 - LINES, NZ), -1.0, F32)], axis=0
+    )
+    shifted = jnp.concatenate(
+        [jnp.full((64, NZ), -1.0, F32), turned[0:64]], axis=0
+    )
+    late = lax.broadcasted_iota(jnp.int32, (128, NZ), 1) % 4 >= 2
+    lines_ref[...] = turned.T.astype(jnp.int32)
+    lines2_ref[...] = jnp.where(late, shifted, turned).T.astype(jnp.int32)
     load_k.wait()
     y_rows = lax.broadcasted_iota(jnp.int32, (NY, 128), 0)
 
@@ -171,8 +204,6 @@
         return 0
 
     lax.fori_loop(0, NS, pack_k, 0, unroll=4)
-
-    pl.semaphore_wait(barrier, NS - 1 + NCOIL - 1)
 
     def spread_out(src, dst, s_sem, r_sem):
         pltpu.make_async_copy(src.at[me], dst.at[me], r_sem).start()
@@ -191,6 +222,7 @@
 
         lax.fori_loop(1, NS, send, 0)
 
+    pl.semaphore_wait(barrier, NS - 1 + NCOIL - 1 + 9)
     spread_out(ksend, krecv, k_s, k_r)
 
     load_c.wait()
@@ -206,13 +238,16 @@
     lax.fori_loop(0, ZL, cot_y, 0)
 
     def pack_c(x, _):
-        for j in range(5):
-            lanes = slice(j * 128, (j + 1) * 128)
-            csend[x, :, lanes] = csc[j, pl.ds(x, 16, stride=NS), :].astype(BF)
+        for n, (lo, hi) in enumerate(GROUPS):
+            for j in range(lo, hi):
+                lanes = slice((j - lo) * 128, (j - lo + 1) * 128)
+                csend[n][x, :, lanes] = csc[j, pl.ds(x, 16, stride=NS), :].astype(BF)
         return 0
 
     lax.fori_loop(0, NS, pack_c, 0, unroll=2)
-    spread_out(csend, crecv, c_s, c_r)
+
+    for n in range(len(GROUPS)):
+        spread_out(csend[n], crecv[n], c_s.at[n], c_r.at[n])
 
     for load in loads[1:]:
         load.wait()
@@ -231,12 +266,18 @@
 
     lax.fori_loop(0, NZ // 32, find, 0)
 
-    w1 = w1m_ref[...]
-    w2 = w2m_ref[...]
+    wt[...] = jnp.zeros((2, 128, 128), F32)
+    for n, ref in enumerate((first_ref, second_ref)):
+        for a in range(3):
+            for b in range(3):
+                at = (a * 3 + b) * 2
+                wt[n, at : at + 2, 0:CH] = ref[a, b].astype(F32)
+    w1 = wt[0].astype(BF)
+    w2 = wt[1].astype(BF)
     sp = spread[...]
     spt = spread_t[...]
-    by_hidden1 = mm(sp, w1).astype(BF)
-    by_hidden2 = mm(sp, w2).astype(BF)
+    by_hidden1 = mm_nt(sp, w1).astype(BF)
+    by_hidden2 = mm_nt(sp, w2).astype(BF)
     band1 = jnp.zeros((MR, KR), F32)
     band2 = jnp.zeros((MR, KR), F32)
     for b in range(3):
@@ -250,12 +291,16 @@
         out1 = jnp.zeros((64, MR), F32)
         for b in range(3):
             hit = gap2[...] == float(b)
-            out2 += jnp.where(hit, mm(mm_nt(rowpick[a * 3 + b], w2).astype(BF), spt), 0.0)
+            out2 += jnp.where(hit, mm(mm(rowpick[a * 3 + b], w2).astype(BF), spt), 0.0)
             flipped = rowpick[(2 - a) * 3 + (2 - b)]
-            out1 += jnp.where(hit, mm(mm_nt(flipped, w1).astype(BF), spt), 0.0)
+            out1 += jnp.where(hit, mm(mm(flipped, w1).astype(BF), spt), 0.0)
         w2b[a] = out2.astype(BF)
         w1f[a] = out1.astype(BF)
-    bias = jnp.sum(sp.astype(F32) * b1_ref[...], axis=1, keepdims=True)
+    lane = lax.broadcasted_iota(jnp.int32, (1, 128), 1)
+    row = jnp.zeros((1, 128), F32)
+    for ch in range(CH):
+        row = jnp.where(lane == ch, b1_ref[ch], row)
+    bias = jnp.sum(sp.astype(F32) * row, axis=1, keepdims=True)
     bcol[...] = jnp.broadcast_to(bias, (MR, 128))
     zero_rows = jnp.zeros((KR - 6 * US, 3 * LN), BF)
     for n in range(2):
@@ -266,19 +311,17 @@
             tmp[j, i, 176:TR, :] = jnp.zeros((TR - 176, 128), F32)
     load_s.wait()
 
-    def to_image(n):
-        def one_coil(c, _):
-            for j in range(5):
-                block = hsc[j, pl.ds(c, NZ, stride=CL), :]
-                ht[j * 128 : (j + 1) * 128, :] = block.T.astype(BF)
-            both = jnp.concatenate([ht[0:NY, :], ht[NY:, :]], axis=1)
-            img[n, c] = mm(both, tz[...]).astype(BF)
-            return 0
-
-        lax.fori_loop(0, CL, one_coil, 0)
+    def to_image(n, j):
+        columns = []
+        for c in range(CL):
+            block = hsc[j, pl.ds(c, NZ, stride=CL), :].T.astype(BF)
+            columns.append(jnp.concatenate([block[0:64], block[64:128]], axis=1))
+        image = mm(jnp.concatenate(columns, axis=0), tz[...]).astype(BF)
+        for c in range(CL):
+            img[n, c, j * 64 : (j + 1) * 64, :] = image[c * 64 : (c + 1) * 64]
 
         def combine(g, _):
-            rows = pl.ds(pl.multiple_of(g * 16, 16), 16)
+            rows = pl.ds(pl.multiple_of(j * 64 + g * 16, 16), 16)
             re = jnp.zeros((16, NZ), F32)
             im = jnp.zeros((16, NZ), F32)
             for c in range(CL):
@@ -294,49 +337,55 @@
             part[n, 1, rows, :] = im.astype(BF)
             return 0
 
-        lax.fori_loop(0, NY // 16, combine, 0)
-
-    def piece(n, to):
-        return part.at[
-            n,
-            :,
-            pl.ds(pl.multiple_of((to % 2) * 144, 16), PR),
-            pl.ds(pl.multiple_of((to // 2) * 128, 128), 128),
-        ]
-
-    def coil_send(n):
-        pltpu.make_async_copy(piece(n, co), rsrecv.at[n, co], rs_r.at[n]).start()
-        for j in range(1, NCOIL):
-            to = lax.rem(co + j, NCOIL)
-            pltpu.make_async_remote_copy(
-                src_ref=piece(n, to),
-                dst_ref=rsrecv.at[n, co],
-                send_sem=rs_s.at[n],
-                recv_sem=rs_r.at[n],
-                device_id=(me, to),
-                device_id_type=MESH,
-            ).start()
-
-    def coil_sum(n):
-        pltpu.make_async_copy(rsrecv.at[n], rsrecv.at[n], rs_r.at[n]).wait()
+        lax.fori_loop(0, 4, combine, 0)
+
+    def coil_send(n, chunk):
+        for j, half, row, count, step in PIECES:
+            if j != chunk:
+                continue
+            for half_z in range(2):
+                to = half_z * 2 + half
+                src = part.at[n, :, pl.ds(row, count), pl.ds(half_z * 128, 128)]
+                dst = rsrecv.at[n, co, :, pl.ds(row - half * 144, count)]
+
+                @pl.when(co == to)
+                def _():
+                    pltpu.make_async_copy(src, dst, rs_r.at[n, step]).start()
+
+                @pl.when(co != to)
+                def _():
+                    pltpu.make_async_remote_copy(
+                        src_ref=src,
+                        dst_ref=dst,
+                        send_sem=rs_s.at[n, step],
+                        recv_sem=rs_r.at[n, step],
+                        device_id=(me, to),
+                        device_id_type=MESH,
+                    ).start()
+
+    def coil_sum(n, step):
+        first, count = STEPS[step]
+        rows = slice(first, first + count)
+        arrived(rsrecv.at[n, :, :, pl.ds(first, count)], rs_r.at[n, step])
         for q in range(2):
-            total = rsrecv[n, 0, q].astype(F32)
+            total = rsrecv[n, 0, q, rows].astype(F32)
             for j in range(1, NCOIL):
-                total += rsrecv[n, j, q].astype(F32)
-            hrecv[n, 4, q] = total.astype(BF)
+                total += rsrecv[n, j, q, rows].astype(F32)
+            hrecv[n, 4, q, rows] = total.astype(BF)
         for slot, off in enumerate((-2, -1, 1, 2)):
             to = lax.rem(me + off + NS, NS)
             pltpu.make_async_remote_copy(
-                src_ref=hrecv.at[n, 4],
-                dst_ref=hrecv.at[n, 3 - slot],
-                send_sem=h_s.at[n],
-                recv_sem=h_r.at[n],
+                src_ref=hrecv.at[n, 4, :, pl.ds(first, count)],
+                dst_ref=hrecv.at[n, 3 - slot, :, pl.ds(first, count)],
+                send_sem=h_s.at[n, step],
+                recv_sem=h_r.at[n, step],
                 device_id=(to, co),
                 device_id_type=MESH,
             ).start()
 
     def windows(n):
-        pltpu.make_async_copy(hrecv.at[n, pl.ds(0, 4)], hrecv.at[n, pl.ds(0, 4)], h_r.at[n]).wait()
+        for step, (first, count) in enumerate(STEPS):
+            arrived(hrecv.at[n, pl.ds(0, 4), :, pl.ds(first, count)], h_r.at[n, step])
         for j, slot in enumerate((0, 1, 4, 2, 3)):
             x = me + j - 2
             inside = jnp.logical_and(x >= 0, x < NS)
@@ -385,7 +434,43 @@
                 device_id_type=MESH,
             ).start()
 
-    pltpu.make_async_copy(krecv, krecv, k_r).wait()
+    def second_grad():
+        rows_b[...] = jnp.zeros((24, MR), F32)
+        own = jnp.concatenate(
+            [
+                jnp.concatenate(
+                    [
+                        hrecv[1, 4, q, pl.ds(pl.multiple_of(hy * 16, 16) + blk * BLK, BLK), :]
+                        for blk in range(NB)
+                    ],
+                    axis=1,
+                )
+                for q in range(2)
+            ],
+            axis=0,
+        )
+        for a in range(3):
+            cross = mm_nt(own, act[:, a * LN : (a + 1) * LN])
+            for q in range(2):
+                rows = slice(q * BLK, (q + 1) * BLK)
+                for b in range(3):
+                    at = a * 6 + b * 2 + q
+                    rows_b[at : at + 1, :] = jnp.sum(
+                        jnp.where(gap2[rows, :] == float(b), cross[rows, :], 0.0),
+                        axis=0,
+                        keepdims=True,
+                    )
+        high = lax.Precision.HIGHEST
+        grads = jnp.dot(rows_b[...], sel_b[...], precision=high, preferred_element_type=F32)
+        at_row = lax.broadcasted_iota(jnp.int32, (24, 128), 0)
+        at_lane = lax.broadcasted_iota(jnp.int32, (24, 128), 1)
+        own_f = own.astype(F32)
+        for q in range(2):
+            spot = jnp.logical_and(at_row == 18, at_lane == 32 + q)
+            grads += jnp.where(spot, jnp.sum(own_f[q * BLK : (q + 1) * BLK]), 0.0)
+        gsec[...] = grads
+
+    arrived(krecv, k_r)
     low_rows = lax.broadcasted_iota(jnp.int32, (8, MR), 0) < 4
     low_lanes = lax.broadcasted_iota(jnp.int32, (8, 128), 1) < 64
 
@@ -430,9 +515,23 @@
         return 0
 
     lax.fori_loop(0, 4, k_y, 0)
-    to_image(0)
-    coil_send(0)
-    coil_sum(0)
+    for j in range(NCH):
+        to_image(0, j)
+        coil_send(0, j)
+
+    def take_cot(n):
+        lo, hi = GROUPS[n]
+        arrived(crecv[n], c_r.at[n])
+        for j in range(lo, hi):
+            lanes = slice((j - lo) * 128, (j - lo + 1) * 128)
+            hsc[j] = crecv[n][:, :, lanes].astype(F32).reshape(16 * NS, 128)
+            to_image(1, j)
+            coil_send(1, j)
+
+    take_cot(0)
+    coil_sum(0, 0)
+    coil_sum(0, 1)
+    take_cot(1)
     windows(0)
     into_hidden(0, w1b)
 
@@ -457,18 +556,34 @@
             agsend[0, q, blk * BLK : (blk + 1) * BLK, :] = block.astype(BF)
     gather_send(0)
 
-    pltpu.make_async_copy(crecv, crecv, c_r).wait()
-
-    def widen(s, _):
-        got = crecv[s].astype(F32)
-        for j in range(5):
-            hsc[j, pl.ds(pl.multiple_of(s * 16, 16), 16), :] = got[:, j * 128 : (j + 1) * 128]
-        return 0
-
-    lax.fori_loop(0, NS, widen, 0, unroll=4)
-    to_image(1)
-    coil_send(1)
-    coil_sum(1)
+    coil_sum(1, 0)
+    take_cot(2)
+    coil_sum(1, 1)
+    second_grad()
+
+    arrived(agrecv.at[0], ag_r.at[0])
+
+    def quarters(g):
+        for half_y in range(2):
+            for half_z in range(2):
+                src = pl.ds(pl.multiple_of(g * 16, 16), 16)
+                dst = pl.ds(pl.multiple_of(half_y * 160 + g * 16, 16), 16)
+                lo = slice(half_z * 128, half_z * 128 + 128)
+                hi = slice(NZ + half_z * 128, NZ + half_z * 128 + 128)
+                yield half_z * 2 + half_y, src, dst, lo, hi
+
+    def begin(g, _):
+        for slot, src, dst, lo, hi in quarters(g):
+            r0 = agrecv[0, slot, 0, src, :].astype(F32)
+            r1 = agrecv[0, slot, 1, src, :].astype(F32)
+            for c in range(CL):
+                k0 = img[1, c, dst, lo].astype(F32)
+                k1 = img[1, c, dst, hi].astype(F32)
+                regpart[0, c, dst, lo] = k0 * r0 + k1 * r1
+                regpart[1, c, dst, lo] = k1 * r0 - k0 * r1
+        return 0
+
+    lax.fori_loop(0, 10, begin, 0)
     windows(1)
     into_hidden(1, w2f)
 
@@ -491,7 +606,6 @@
     gather_send(1)
 
     rows_a[...] = jnp.zeros((24, MR), F32)
-    rows_b[...] = jnp.zeros((24, MR), F32)
     gp_mid = gp[:, LN : 2 * LN]
     cross = mm_nt(vbuf[0, :, LN : 2 * LN], gp_mid)
     for i in range(2):
@@ -500,46 +614,15 @@
             block = cross[rows, :]
             gap = gap3[rows, :]
             for b in range(3):
-                at = i * 9 + a * 3 + b
+                at = (a * 3 + b) * 2 + i
                 rows_a[at : at + 1, :] = jnp.sum(
                     jnp.where(gap == float(b), block, 0.0), axis=0, keepdims=True
                 )
     sums = mm_nt(jnp.ones((8, LN), BF), gp_mid) * middle[...]
     rows_a[18:19, :] = sums[0:1, :]
-    own = jnp.concatenate(
-        [
-            jnp.concatenate(
-                [
-                    hrecv[1, 4, q, pl.ds(pl.multiple_of(hy * 16, 16) + blk * BLK, BLK), :]
-                    for blk in range(NB)
-                ],
-                axis=1,
-            )
-            for q in range(2)
-        ],
-        axis=0,
-    )
-    for a in range(3):
-        cross = mm_nt(own, act[:, a * LN : (a + 1) * LN])
-        for q in range(2):
-            rows = slice(q * BLK, (q + 1) * BLK)
-            for b in range(3):
-                at = a * 6 + b * 2 + q
-                rows_b[at : at + 1, :] = jnp.sum(
-                    jnp.where(gap2[rows, :] == float(b), cross[rows, :], 0.0),
-                    axis=0,
-                    keepdims=True,
-                )
     high = lax.Precision.HIGHEST
     grads = jnp.dot(rows_a[...], sel_a[...], precision=high, preferred_element_type=F32)
-    grads += jnp.dot(rows_b[...], sel_b[...], precision=high, preferred_element_type=F32)
-    at_row = lax.broadcasted_iota(jnp.int32, (24, 128), 0)
-    at_lane = lax.broadcasted_iota(jnp.int32, (24, 128), 1)
-    own_f = own.astype(F32)
-    for q in range(2):
-        spot = jnp.logical_and(at_row == 18, at_lane == 32 + q)
-        grads += jnp.where(spot, jnp.sum(own_f[q * BLK : (q + 1) * BLK]), 0.0)
-
+    grads += gsec[...]
     def share(n, buf, count, mine, device):
         buf[mine] = grads_in[n]
         for j in range(1, count):
@@ -554,74 +637,90 @@
             ).start()
 
     def collect(n, buf, count):
-        rest_of = buf.at[pl.ds(0, count - 1)]
-        pltpu.make_async_copy(rest_of, rest_of, ar_r.at[n]).wait()
+        arrived(buf.at[pl.ds(0, count - 1)], ar_r.at[n])
         total = buf[0]
         for j in range(1, count):
             total += buf[j]
         return total
 
-    row_y, row_zc = me // 16, me % 16
     grads_in = [grads]
     share(0, ar1, 16, row_zc, lambda to: (row_y * 16 + to, co))
 
-    pltpu.make_async_copy(agrecv.at[0], agrecv.at[0], ag_r.at[0]).wait()
-    pltpu.make_async_copy(agrecv.at[1], agrecv.at[1], ag_r.at[1]).wait()
-
-    def finish(g, _):
-        for half_y in range(2):
-            for half_z in range(2):
-                slot = half_z * 2 + half_y
-                src = pl.ds(pl.multiple_of(g * 16, 16), 16)
-                dst = pl.ds(pl.multiple_of(half_y * 160 + g * 16, 16), 16)
-                lo = slice(half_z * 128, half_z * 128 + 128)
-                hi = slice(NZ + half_z * 128, NZ + half_z * 128 + 128)
-                r0 = agrecv[0, slot, 0, src, :].astype(F32)
-                r1 = agrecv[0, slot, 1, src, :].astype(F32)
+    arrived(agrecv.at[1], ag_r.at[1])
+
+    def result(half):
+        def finish(g, _):
+            for slot, src, dst, lo, hi in quarters(g):
                 g0 = agrecv[1, slot, 0, src, :].astype(F32)
                 g1 = agrecv[1, slot, 1, src, :].astype(F32)
-                for c in range(CL):
+                for c in range(half * 2, half * 2 + 2):
                     i0 = img[0, c, dst, lo].astype(F32)
                     i1 = img[0, c, dst, hi].astype(F32)
-                    k0 = img[1, c, dst, lo].astype(F32)
-                    k1 = img[1, c, dst, hi].astype(F32)
-                    re = -(k0 * r0 + k1 * r1) + i0 * g0 + i1 * g1
-                    im = -(k1 * r0 - k0 * r1) + i1 * g0 - i0 * g1
-                    out_ref[0, c, dst, lo] = re.astype(BF)
-                    out_ref[1, c, dst, lo] = im.astype(BF)
-        return 0
-
-    lax.fori_loop(0, 10, finish, 0)
+                    re = i0 * g0 + i1 * g1 - regpart[0, c, dst, lo]
+                    im = i1 * g0 - i0 * g1 - regpart[1, c, dst, lo]
+                    outv[0, c, dst, lo] = re.astype(BF)
+                    outv[1, c, dst, lo] = im.astype(BF)
+            return 0
+
+        lax.fori_loop(0, 10, finish, 0)
+        for p in range(2):
+            store(p, half).start()
+
+    def store(p, half):
+        coils = pl.ds(half * 2, 2)
+        return pltpu.make_async_copy(
+            outv.at[p, coils], pre_hbm.at[p, coils], o_sem.at[p * 2 + half]
+        )
+
+    result(0)
 
     grads_in.append(collect(0, ar1, 16))
-    share(1, ar2, 4, row_y, lambda to: (to * 16 + row_zc, co))
-    grads_in.append(collect(1, ar2, 4))
-    share(2, ar3, 4, co, lambda to: (me, to))
-    gw_ref[...] = collect(2, ar3, 4) * (1.0 / math.sqrt(NS * NY * NZ))
-
-    def sent(ref, sem):
-        pltpu.make_async_copy(ref, ref, sem).wait()
-
-    sent(ksend.at[pl.ds(0, NS - 1)], k_s)
-    sent(csend.at[pl.ds(0, NS - 1)], c_s)
+    share(1, ar2, 16, row_y * 4 + co, lambda to: (to // 4 * 16 + row_zc, to % 4))
+    result(1)
+    gw_ref[...] = collect(1, ar2, 16) * (1.0 / math.sqrt(NS * NY * NZ))
+
+    arrived(ksend.at[pl.ds(0, NS - 1)], k_s)
+    for n in range(len(GROUPS)):
+        arrived(csend[n].at[pl.ds(0, NS - 1)], c_s.at[n])
     for n in range(2):
-        sent(rsrecv.at[n, pl.ds(0, NCOIL - 1)], rs_s.at[n])
-        sent(hrecv.at[n, pl.ds(0, 4)], h_s.at[n])
-        sent(agrecv.at[n, pl.ds(0, NCOIL - 1)], ag_s.at[n])
-    sent(ar1.at[pl.ds(0, 15)], ar_s.at[0])
-    sent(ar2.at[pl.ds(0, 3)], ar_s.at[1])
-    sent(ar3.at[pl.ds(0, 3)], ar_s.at[2])
+        for step, (first, count) in enumerate(STEPS):
+            arrived(rsrecv.at[n, pl.ds(0, 3), :, pl.ds(first, count)], rs_s.at[n, step])
+            arrived(hrecv.at[n, pl.ds(0, 4), :, pl.ds(first, count)], h_s.at[n, step])
+        arrived(agrecv.at[n, pl.ds(0, NCOIL - 1)], ag_s.at[n])
+    arrived(ar1.at[pl.ds(0, 15)], ar_s.at[0])
+    arrived(ar2.at[pl.ds(0, 15)], ar_s.at[1])
+    for p in range(2):
+        for half in range(2):
+            store(p, half).wait()
+
+
+def final_kernel(pre_hbm, gw_ref, out_hbm, g1_ref, gb1_ref, g2_ref, gb2_ref, held, sem_in, sem_out):
+    spots = [(p, c) for p in range(2) for c in range(CL)]
+    loads = [pltpu.make_async_copy(pre_hbm.at[s], held.at[s], sem_in.at[s]) for s in spots]
+    stores = [pltpu.make_async_copy(held.at[s], out_hbm.at[s], sem_out.at[s]) for s in spots]
+    for load in loads:
+        load.start()
+    second = pltpu.roll(gw_ref[...], 96, 1)
+    for a in range(3):
+        for b in range(3):
+            at = (a * 3 + b) * 2
+            g1_ref[a, b] = gw_ref[at : at + 2, 0:CH]
+            g2_ref[a, b] = second[at : at + 2, 0:CH]
+    gb1_ref[...] = gw_ref[18:19, 0:CH]
+    gb2_ref[...] = second[18:19, 0:2]
+    for load, store in zip(loads, stores):
+        load.wait()
+        store.start()
+    for store in stores:
+        store.wait()
 
 
 def on_device(k_space, cotangent, sens_maps, line_index, w_first, b_first, w_second, b_second):
     constants = make_constants()
     sens = jnp.transpose(sens_maps.reshape(2, CL, NZ, NY), (0, 1, 3, 2))
-    lines = jnp.pad(line_index, ((0, 0), (0, 128 - LINES)), constant_values=-1)
-    upper = (jnp.arange(NZ) % 4 >= 2)[:, None]
-    lines2 = jnp.where(upper, jnp.roll(lines, 64, axis=1), lines)
-    w1m = jnp.pad(w_first.reshape(CH, 18), ((0, 128 - CH), (0, 110)))
-    w2m = jnp.pad(jnp.transpose(w_second, (1, 0, 2, 3)).reshape(CH, 18), ((0, 128 - CH), (0, 110)))
-    b1 = jnp.pad(b_first, (0, 110)).reshape(1, 128)
+    index = jnp.transpose(line_index)
+    first = jnp.transpose(w_first, (2, 3, 1, 0))
+    second = jnp.transpose(w_second, (2, 3, 0, 1))
     vm = pl.BlockSpec(memory_space=pltpu.VMEM)
     anym = pl.BlockSpec(memory_space=pl.ANY)
     dma = pltpu.SemaphoreType.DMA
@@ -634,12 +733,11 @@
         pltpu.VMEM((NS, 16, 128), BF),
         pltpu.VMEM((NS, 16, 128), BF),
         pltpu.VMEM((5, 16 * NS, 128), F32),
-        pltpu.VMEM((NS, 16, 640), BF),
-        pltpu.VMEM((NS, 16, 640), BF),
+        *[pltpu.VMEM((NS, 16, 128 * (hi - lo)), BF) for lo, hi in GROUPS],
+        *[pltpu.VMEM((NS, 16, 128 * (hi - lo)), BF) for lo, hi in GROUPS],
         pltpu.VMEM((NZ, 640), jnp.int32),
         pltpu.VMEM((NZ * CL, 640), BF),
         pltpu.VMEM((5, NZ * CL, 128), F32),
-        pltpu.VMEM((640, NZ), BF),
         pltpu.VMEM((2, CL, NY, 2 * NZ), BF),
         pltpu.VMEM((2, 2, NY, NZ), BF),
         pltpu.VMEM((2, NCOIL, 2, PR, 128), BF),
@@ -656,47 +754,65 @@
         pltpu.VMEM((3, 64, MR), BF),
         pltpu.VMEM((2, 2, NY // 2, 128), BF),
         pltpu.VMEM((2, NCOIL, 2, NY // 2, 128), BF),
+        pltpu.VMEM((2, CL, NY, NZ), F32),
+        pltpu.VMEM((2, CL, NY, NZ), BF),
         pltpu.VMEM((24, MR), F32),
         pltpu.VMEM((24, MR), F32),
+        pltpu.VMEM((24, 128), F32),
         pltpu.VMEM((16, 24, 128), F32),
-        pltpu.VMEM((4, 24, 128), F32),
-        pltpu.VMEM((4, 24, 128), F32),
+        pltpu.VMEM((16, 24, 128), F32),
+        pltpu.VMEM((NZ, 128), jnp.int32),
+        pltpu.VMEM((NZ, 128), jnp.int32),
+        pltpu.VMEM((2, 128, 128), F32),
         dma((3,)),
         dma((len(constants),)),
+        dma((4,)),
         dma,
         dma,
-        dma,
-        dma,
+        dma((len(GROUPS),)),
+        dma((len(GROUPS),)),
+        dma((2, 2)),
+        dma((2, 2)),
+        dma((2, 2)),
+        dma((2, 2)),
         dma((2,)),
         dma((2,)),
         dma((2,)),
         dma((2,)),
-        dma((2,)),
-        dma((2,)),
-        dma((3,)),
-        dma((3,)),
     ]
-    grad_sens, grads = pl.pallas_call(
+    smem = pl.BlockSpec(memory_space=pltpu.SMEM)
+    result, grads = pl.pallas_call(
         cascade_kernel,
         out_shape=(
             jax.ShapeDtypeStruct((2, CL, NY, NZ), BF),
             jax.ShapeDtypeStruct((24, 128), F32),
         ),
-        in_specs=[anym] * 3
-        + [vm] * 5
-        + [pl.BlockSpec(memory_space=pltpu.SMEM)]
-        + [anym] * len(constants),
-        out_specs=(vm, vm),
+        in_specs=[anym] * 3 + [vm] * 3 + [smem] * 2 + [anym] * len(constants),
+        out_specs=(anym, vm),
         scratch_shapes=scratch,
         compiler_params=pltpu.CompilerParams(
             collective_id=0, has_side_effects=True, vmem_limit_bytes=60 * 1024 * 1024
         ),
-    )(k_space, cotangent, sens, lines, lines2, w1m, w2m, b1, b_second, *constants)
+    )(k_space, cotangent, sens, index, first, second, b_first, b_second, *constants)
+    grad_sens, grad_w1, grad_b1, grad_w2, grad_b2 = pl.pallas_call(
+        final_kernel,
+        out_shape=(
+            jax.ShapeDtypeStruct((2, CL, NY, NZ), BF),
+            jax.ShapeDtypeStruct((3, 3, 2, CH), F32),
+            jax.ShapeDtypeStruct((1, CH), F32),
+            jax.ShapeDtypeStruct((3, 3, 2, CH), F32),
+            jax.ShapeDtypeStruct((1, 2), F32),
+        ),
+        in_specs=[anym, vm],
+        out_specs=(anym, vm, vm, vm, vm),
+        scratch_shapes=[pltpu.VMEM((2, CL, NY, NZ), BF), dma((2, CL)), dma((2, CL))],
+        compiler_params=pltpu.CompilerParams(vmem_limit_bytes=60 * 1024 * 1024),
+    )(result, grads)
     grad_sens = jnp.transpose(grad_sens, (0, 1, 3, 2)).reshape(2, CL, NZ, 1, NY)
-    grad_w1 = jnp.transpose(grads[0:18, 0:CH]).reshape(CH, 2, 3, 3)
-    grad_b1 = grads[18, 0:CH]
-    grad_w2 = jnp.transpose(grads[0:18, 32 : 32 + CH].reshape(3, 3, 2, CH), (2, 3, 0, 1))
-    grad_b2 = grads[18, 32:34]
+    grad_w1 = jnp.transpose(grad_w1, (3, 2, 0, 1))
+    grad_w2 = jnp.transpose(grad_w2, (2, 3, 0, 1))
+    grad_b1 = grad_b1.reshape(CH)
+    grad_b2 = grad_b2.reshape(2)
     return (grad_sens, grad_w1, grad_b1, grad_w2, grad_b2)
 
 

time: 105 us -> 87.8 us (0.84); the launches traced: 103 us -> 87.6 us
  local copies, waits for them, and re-layouts: 11.9 us -> 0 us
  Pallas kernels: 90 us -> 86.8 us
    pallas_call x1, Pallas kernels: 90 us -> 83.3 us  [on_device(): pl.pallas_call(cascade_kernel, out_shape=(jax.ShapeDtypeStruct((2, CL, NY...]
    unnamed x4 -> x0, local copies, waits for them, and re-layouts: 4.62 us -> none
    pallas_call x0 -> x1, Pallas kernels: none -> 3.52 us  [on_device(): pl.pallas_call(final_kernel, out_shape=(jax.ShapeDtypeStruct((2, CL, NY,...]
    squeeze x2 -> x0, local copies, waits for them, and re-layouts: 2.46 us -> none  [the longest x1 1.26 us: on_device(): grad_b2 = grads[18, 32:34]]
    reshape x7 -> x0, local copies, waits for them, and re-layouts: 2.04 us -> none  [the longest x1 1.17 us: on_device(): b1 = jnp.pad(b_first, (0, 110)).reshape(1, 128)]
    pad x2 -> x0, local copies, waits for them, and re-layouts: 1.25 us -> none  [the longest x1 0.62 us: on_device(): jnp.pad(jnp.transpose(w_second, (1, 0, 2, 3)).reshape(CH, 18), ((0, 128 -...]
where the time goes in v2:
time: 87.8 us; the launch traced here: 87.6 us
  Pallas kernels  86.8 us (99%)
    pallas_call x1, Pallas kernels, on_device(): pl.pallas_call(cascade_kernel, out_shape=(jax.ShapeDtypeStruct((2, CL, NY...  83.3 us
    pallas_call x1, Pallas kernels, on_device(): pl.pallas_call(final_kernel, out_shape=(jax.ShapeDtypeStruct((2, CL, NY,...  3.52 us

profile of v2, /device:TPU:1, one launch (start us, length us, event | category | flops | bytes accessed | tf_op | source)
XLA Modules:
  0.0 87.6 jit_solution(7219368164814409043)
XLA Ops:
  0.6 83.3 %shard_map.245 = (bf16[2,4,320,256]{3,2,1,0:T(8,128)(2,1)}, f32[24,128]{1,0:T(8,128)}) custom-call(bf16[2,4,4,64,320]{4,3,2,1,0:T(8,128)(2,1)} %refs_0_.1, bf16[2,4,4,64,320]{4,3,2,1,0:T(8,128)(2,1)} %refs_1_.1, bf16[2,4,320,256]{3,2,1,0:T(8,128)(2,1)} %bitcast.15, s32[40,256]{1,0:T(8,128)} %bitcast.16, bf16[3,3,2,18]{3,2,1,0:T(2,128)(2,1)} %bitcast.17, ...), custom_call_target="tpu_custom_call" | custom-call | tf_op jit(solution)/shard_map/pallas_call | solution.py:784
  83.9 3.5 %shard_map.246 = (bf16[2,4,320,256]{3,2,1,0:T(8,128)(2,1)}, f32[3,3,2,18]{3,2,1,0:T(2,128)}, f32[1,18]{1,0:T(1,128)}, f32[3,3,2,18]{3,2,1,0:T(2,128)}, f32[1,2]{1,0:T(1,128)}) custom-call(bf16[2,4,320,256]{3,2,1,0:T(8,128)(2,1)} %get-tuple-element.12.pre_hbm, f32[24,128]{1,0:T(8,128)} %get-tuple-element.13.gw_ref), custom_call_target="tpu_custom_call" | custom-call | tf_op jit(solution)/shard_map/pallas_call | solution.py:797

commit v3 on v2

--- a/solution.py
+++ b/solution.py
@@ -32,6 +32,7 @@
     (3, 1, 192, 64, 0),
     (4, 1, 256, 64, 1),
 )
+BLOCKS = ((0, 2), (2, 5))
 STEPS = ((0, 112), (112, 64))
 
 
@@ -89,7 +90,7 @@
         inner[r] = 1 <= v <= BLK
     gap3 = np.where(inner[None, :], gap1.T, 99.0).astype(np.float32)
     sel_a = spread
-    sel_b = np.roll(spread, 32, axis=1)
+    sel_b = np.roll(spread, CH, axis=1)
     middle = np.broadcast_to(inner[None, :], (8, MR)).astype(np.float32)
     edge = np.zeros((MR, 128), np.float32)
     for r, _, v in hid:
@@ -265,6 +266,237 @@
         return 0
 
     lax.fori_loop(0, NZ // 32, find, 0)
+
+    load_s.wait()
+
+    def to_image(n, j):
+        columns = []
+        for c in range(CL):
+            block = hsc[j, pl.ds(c, NZ, stride=CL), :].T.astype(BF)
+            columns.append(jnp.concatenate([block[0:64], block[64:128]], axis=1))
+        image = mm(jnp.concatenate(columns, axis=0), tz[...]).astype(BF)
+        for c in range(CL):
+            img[n, c, j * 64 : (j + 1) * 64, :] = image[c * 64 : (c + 1) * 64]
+
+        def combine(g, _):
+            rows = pl.ds(pl.multiple_of(j * 64 + g * 16, 16), 16)
+            re = jnp.zeros((16, NZ), F32)
+            im = jnp.zeros((16, NZ), F32)
+            for c in range(CL):
+                both = img[n, c, rows, :].astype(F32)
+                i0, i1 = both[:, :NZ], both[:, NZ:]
+                s0 = sv[0, c, rows, :].astype(F32)
+                s1 = sv[1, c, rows, :].astype(F32)
+                re += s0 * i0 + s1 * i1
+                im += s0 * i1 - s1 * i0
+            if n == 1:
+                re, im = -re, -im
+            part[n, 0, rows, :] = re.astype(BF)
+            part[n, 1, rows, :] = im.astype(BF)
+            return 0
+
+        lax.fori_loop(0, 4, combine, 0)
+
+    def coil_send(n, chunk):
+        for j, half, row, count, step in PIECES:
+            if j != chunk:
+                continue
+            for half_z in range(2):
+                to = half_z * 2 + half
+                src = part.at[n, :, pl.ds(row, count), pl.ds(half_z * 128, 128)]
+                dst = rsrecv.at[n, co, :, pl.ds(row - half * 144, count)]
+
+                @pl.when(co == to)
+                def _():
+                    pltpu.make_async_copy(src, dst, rs_r.at[n, step]).start()
+
+                @pl.when(co != to)
+                def _():
+                    pltpu.make_async_remote_copy(
+                        src_ref=src,
+                        dst_ref=dst,
+                        send_sem=rs_s.at[n, step],
+                        recv_sem=rs_r.at[n, step],
+                        device_id=(me, to),
+                        device_id_type=MESH,
+                    ).start()
+
+    def coil_sum(n, step):
+        first, count = STEPS[step]
+        rows = slice(first, first + count)
+        arrived(rsrecv.at[n, :, :, pl.ds(first, count)], rs_r.at[n, step])
+        for q in range(2):
+            total = rsrecv[n, 0, q, rows].astype(F32)
+            for j in range(1, NCOIL):
+                total += rsrecv[n, j, q, rows].astype(F32)
+            hrecv[n, 4, q, rows] = total.astype(BF)
+        for slot, off in enumerate((-2, -1, 1, 2)):
+            to = lax.rem(me + off + NS, NS)
+            pltpu.make_async_remote_copy(
+                src_ref=hrecv.at[n, 4, :, pl.ds(first, count)],
+                dst_ref=hrecv.at[n, 3 - slot, :, pl.ds(first, count)],
+                send_sem=h_s.at[n, step],
+                recv_sem=h_r.at[n, step],
+                device_id=(to, co),
+                device_id_type=MESH,
+            ).start()
+
+    def windows(n, step):
+        first, count = STEPS[step]
+        arrived(hrecv.at[n, pl.ds(0, 4), :, pl.ds(first, count)], h_r.at[n, step])
+        for j, slot in enumerate((0, 1, 4, 2, 3)):
+            x = me + j - 2
+            inside = jnp.logical_and(x >= 0, x < NS)
+            for q in range(2):
+                got = hrecv[n, slot, q, first : first + count].astype(F32)
+                tmp[j, q, 2 + first : 2 + first + count, :] = jnp.where(inside, got, 0.0)
+        for x3 in range(3):
+            for blk in range(*BLOCKS[step]):
+                lanes = slice((x3 * NB + blk) * 128, (x3 * NB + blk + 1) * 128)
+                rows = pl.ds(pl.multiple_of(hy * 16, 16) + blk * BLK, US)
+                column = [tmp[x3 + a, q, rows, :] for q in range(2) for a in range(3)]
+                vbuf[n, 0 : 6 * US, lanes] = jnp.concatenate(column, axis=0).astype(BF)
+
+    def lanes_of(x3, step):
+        lo, hi = BLOCKS[step]
+        return slice(x3 * LN + lo * 128, x3 * LN + hi * 128)
+
+    def into_hidden(n, w, step):
+        for x3 in range(3):
+            lanes = lanes_of(x3, step)
+            hid[n, :, lanes] = mm(w[...], vbuf[n, :, lanes])
+
+    x_ok = [jnp.logical_and(me + d >= 0, me + d < NS) for d in (-1, 0, 1)]
+
+    def keep(value, kind, x3, blk):
+        if blk == 0:
+            value = jnp.where(jnp.logical_and(kind == 1.0, hy == 0), 0.0, value)
+        if blk == NB - 1:
+            value = jnp.where(jnp.logical_and(kind == 2.0, hy == 1), 0.0, value)
+        if x3 != 1:
+            value = jnp.where(x_ok[x3], value, 0.0)
+        return value
+
+    def out_of_hidden(values, w, step):
+        total = mm(w[0], values[:, lanes_of(0, step)])
+        total += mm(w[1], values[:, lanes_of(1, step)])
+        total += mm(w[2], values[:, lanes_of(2, step)])
+        return total
+
+    def gather_send(n, step):
+        lo, hi = BLOCKS[step]
+        rows = pl.ds(lo * BLK, (hi - lo) * BLK)
+        src = agsend.at[n, :, rows]
+        dst = agrecv.at[n, co, :, rows]
+        pltpu.make_async_copy(src, dst, ag_r.at[n, step]).start()
+        for j in range(1, NCOIL):
+            to = lax.rem(co + j, NCOIL)
+            pltpu.make_async_remote_copy(
+                src_ref=src,
+                dst_ref=dst,
+                send_sem=ag_s.at[n, step],
+                recv_sem=ag_r.at[n, step],
+                device_id=(me, to),
+                device_id_type=MESH,
+            ).start()
+
+    def gathered(n):
+        for step, (lo, hi) in enumerate(BLOCKS):
+            arrived(agrecv.at[n, :, :, pl.ds(lo * BLK, (hi - lo) * BLK)], ag_r.at[n, step])
+
+    def second_grad():
+        rows_b[...] = jnp.zeros((24, MR), F32)
+        own = jnp.concatenate(
+            [
+                jnp.concatenate(
+                    [
+                        hrecv[1, 4, q, pl.ds(pl.multiple_of(hy * 16, 16) + blk * BLK, BLK), :]
+                        for blk in range(NB)
+                    ],
+                    axis=1,
+                )
+                for q in range(2)
+            ],
+            axis=0,
+        )
+        for a in range(3):
+            cross = mm_nt(own, act[:, a * LN : (a + 1) * LN])
+            for q in range(2):
+                rows = slice(q * BLK, (q + 1) * BLK)
+                for b in range(3):
+                    at = a * 6 + b * 2 + q
+                    rows_b[at : at + 1, :] = jnp.sum(
+                        jnp.where(gap2[rows, :] == float(b), cross[rows, :], 0.0),
+                        axis=0,
+                        keepdims=True,
+                    )
+        high = lax.Precision.HIGHEST
+        grads = jnp.dot(rows_b[...], sel_b[...], precision=high, preferred_element_type=F32)
+        at_row = lax.broadcasted_iota(jnp.int32, (24, 128), 0)
+        at_lane = lax.broadcasted_iota(jnp.int32, (24, 128), 1)
+        own_f = own.astype(F32)
+        for q in range(2):
+            spot = jnp.logical_and(at_row == 18, at_lane == CH + q)
+            grads += jnp.where(spot, jnp.sum(own_f[q * BLK : (q + 1) * BLK]), 0.0)
+        gsec[...] = grads
+
+    arrived(krecv, k_r)
+    low_rows = lax.broadcasted_iota(jnp.int32, (8, MR), 0) < 4
+    low_lanes = lax.broadcasted_iota(jnp.int32, (8, 128), 1) < 64
+
+    def pick(values, index):
+        return jnp.take_along_axis(values, index, axis=1, mode="promise_in_bounds")
+
+    def expand(s, _):
+        got = krecv[s].astype(F32)
+        halves = []
+        for zhi in range(2):
+            first = pos[pl.ds(s * 4 + 2 * zhi, 1), :]
+            second = pos[pl.ds(s * 4 + 2 * zhi + 1, 1), :]
+            index = jnp.where(
+                low_rows,
+                jnp.broadcast_to(first, (8, MR)),
+                jnp.broadcast_to(second, (8, MR)),
+            )
+            at = [index[:, j * 128 : (j + 1) * 128] for j in range(5)]
+            re, im = got[0:8], got[8:16]
+            halves.append(
+                jnp.concatenate(
+                    [
+                        pick(re, at[0]),
+                        pick(re, at[1]),
+                        jnp.where(low_lanes, pick(re, at[2]), pick(im, at[2])),
+                        pick(im, at[3]),
+                        pick(im, at[4]),
+                    ],
+                    axis=1,
+                )
+            )
+        ex[pl.ds(pl.multiple_of(s * 16, 16), 16), :] = jnp.concatenate(halves, axis=0).astype(BF)
+        return 0
+
+    lax.fori_loop(0, NS, expand, 0, unroll=8)
+
+    def k_y(g, _):
+        rows = pl.ds(pl.multiple_of(g * 256, 256), 256)
+        half = mm(ex[rows, :], ty[...]).astype(BF).astype(F32)
+        for j in range(5):
+            hsc[j, rows, :] = half[:, j * 128 : (j + 1) * 128]
+        return 0
+
+    lax.fori_loop(0, 4, k_y, 0)
+    for j in range(NCH):
+        to_image(0, j)
+        coil_send(0, j)
+
+    def take_cot(n):
+        lo, hi = GROUPS[n]
+        arrived(crecv[n], c_r.at[n])
+        for j in range(lo, hi):
+            lanes = slice((j - lo) * 128, (j - lo + 1) * 128)
+            hsc[j] = crecv[n][:, :, lanes].astype(F32).reshape(16 * NS, 128)
+            to_image(1, j)
+            coil_send(1, j)
 
     wt[...] = jnp.zeros((2, 128, 128), F32)
     for n, ref in enumerate((first_ref, second_ref)):
@@ -309,231 +541,16 @@
         for i in range(2):
             tmp[j, i, 0:8, :] = jnp.zeros((8, 128), F32)
             tmp[j, i, 176:TR, :] = jnp.zeros((TR - 176, 128), F32)
-    load_s.wait()
-
-    def to_image(n, j):
-        columns = []
-        for c in range(CL):
-            block = hsc[j, pl.ds(c, NZ, stride=CL), :].T.astype(BF)
-            columns.append(jnp.concatenate([block[0:64], block[64:128]], axis=1))
-        image = mm(jnp.concatenate(columns, axis=0), tz[...]).astype(BF)
-        for c in range(CL):
-            img[n, c, j * 64 : (j + 1) * 64, :] = image[c * 64 : (c + 1) * 64]
-
-        def combine(g, _):
-            rows = pl.ds(pl.multiple_of(j * 64 + g * 16, 16), 16)
-            re = jnp.zeros((16, NZ), F32)
-            im = jnp.zeros((16, NZ), F32)
-            for c in range(CL):
-                both = img[n, c, rows, :].astype(F32)
-                i0, i1 = both[:, :NZ], both[:, NZ:]
-                s0 = sv[0, c, rows, :].astype(F32)
-                s1 = sv[1, c, rows, :].astype(F32)
-                re += s0 * i0 + s1 * i1
-                im += s0 * i1 - s1 * i0
-            if n == 1:
-                re, im = -re, -im
-            part[n, 0, rows, :] = re.astype(BF)
-            part[n, 1, rows, :] = im.astype(BF)
-            return 0
-
-        lax.fori_loop(0, 4, combine, 0)
-
-    def coil_send(n, chunk):
-        for j, half, row, count, step in PIECES:
-            if j != chunk:
-                continue
-            for half_z in range(2):
-                to = half_z * 2 + half
-                src = part.at[n, :, pl.ds(row, count), pl.ds(half_z * 128, 128)]
-                dst = rsrecv.at[n, co, :, pl.ds(row - half * 144, count)]
-
-                @pl.when(co == to)
-                def _():
-                    pltpu.make_async_copy(src, dst, rs_r.at[n, step]).start()
-
-                @pl.when(co != to)
-                def _():
-                    pltpu.make_async_remote_copy(
-                        src_ref=src,
-                        dst_ref=dst,
-                        send_sem=rs_s.at[n, step],
-                        recv_sem=rs_r.at[n, step],
-                        device_id=(me, to),
-                        device_id_type=MESH,
-                    ).start()
-
-    def coil_sum(n, step):
-        first, count = STEPS[step]
-        rows = slice(first, first + count)
-        arrived(rsrecv.at[n, :, :, pl.ds(first, count)], rs_r.at[n, step])
-        for q in range(2):
-            total = rsrecv[n, 0, q, rows].astype(F32)
-            for j in range(1, NCOIL):
-                total += rsrecv[n, j, q, rows].astype(F32)
-            hrecv[n, 4, q, rows] = total.astype(BF)
-        for slot, off in enumerate((-2, -1, 1, 2)):
-            to = lax.rem(me + off + NS, NS)
-            pltpu.make_async_remote_copy(
-                src_ref=hrecv.at[n, 4, :, pl.ds(first, count)],
-                dst_ref=hrecv.at[n, 3 - slot, :, pl.ds(first, count)],
-                send_sem=h_s.at[n, step],
-                recv_sem=h_r.at[n, step],
-                device_id=(to, co),
-                device_id_type=MESH,
-            ).start()
-
-    def windows(n):
-        for step, (first, count) in enumerate(STEPS):
-            arrived(hrecv.at[n, pl.ds(0, 4), :, pl.ds(first, count)], h_r.at[n, step])
-        for j, slot in enumerate((0, 1, 4, 2, 3)):
-            x = me + j - 2
-            inside = jnp.logical_and(x >= 0, x < NS)
-            for q in range(2):
-                got = hrecv[n, slot, q].astype(F32)
-                tmp[j, q, 2 : 2 + PR, :] = jnp.where(inside, got, 0.0)
-        for x3 in range(3):
-            for blk in range(NB):
-                lanes = slice((x3 * NB + blk) * 128, (x3 * NB + blk + 1) * 128)
-                rows = pl.ds(pl.multiple_of(hy * 16, 16) + blk * BLK, US)
-                column = [tmp[x3 + a, q, rows, :] for q in range(2) for a in range(3)]
-                vbuf[n, 0 : 6 * US, lanes] = jnp.concatenate(column, axis=0).astype(BF)
-
-    def into_hidden(n, w):
-        for x3 in range(3):
-            lanes = slice(x3 * LN, (x3 + 1) * LN)
-            hid[n, :, lanes] = mm(w[...], vbuf[n, :, lanes])
-
-    x_ok = [jnp.logical_and(me + d >= 0, me + d < NS) for d in (-1, 0, 1)]
-
-    def keep(value, kind, x3, blk):
-        if blk == 0:
-            value = jnp.where(jnp.logical_and(kind == 1.0, hy == 0), 0.0, value)
-        if blk == NB - 1:
-            value = jnp.where(jnp.logical_and(kind == 2.0, hy == 1), 0.0, value)
-        if x3 != 1:
-            value = jnp.where(x_ok[x3], value, 0.0)
-        return value
-
-    def out_of_hidden(values, w):
-        total = mm(w[0], values[:, 0:LN])
-        total += mm(w[1], values[:, LN : 2 * LN])
-        total += mm(w[2], values[:, 2 * LN :])
-        return total
-
-    def gather_send(n):
-        pltpu.make_async_copy(agsend.at[n], agrecv.at[n, co], ag_r.at[n]).start()
-        for j in range(1, NCOIL):
-            to = lax.rem(co + j, NCOIL)
-            pltpu.make_async_remote_copy(
-                src_ref=agsend.at[n],
-                dst_ref=agrecv.at[n, co],
-                send_sem=ag_s.at[n],
-                recv_sem=ag_r.at[n],
-                device_id=(me, to),
-                device_id_type=MESH,
-            ).start()
-
-    def second_grad():
-        rows_b[...] = jnp.zeros((24, MR), F32)
-        own = jnp.concatenate(
-            [
-                jnp.concatenate(
-                    [
-                        hrecv[1, 4, q, pl.ds(pl.multiple_of(hy * 16, 16) + blk * BLK, BLK), :]
-                        for blk in range(NB)
-                    ],
-                    axis=1,
-                )
-                for q in range(2)
-            ],
-            axis=0,
-        )
-        for a in range(3):
-            cross = mm_nt(own, act[:, a * LN : (a + 1) * LN])
-            for q in range(2):
-                rows = slice(q * BLK, (q + 1) * BLK)
-                for b in range(3):
-                    at = a * 6 + b * 2 + q
-                    rows_b[at : at + 1, :] = jnp.sum(
-                        jnp.where(gap2[rows, :] == float(b), cross[rows, :], 0.0),
-                        axis=0,
-                        keepdims=True,
-                    )
-        high = lax.Precision.HIGHEST
-        grads = jnp.dot(rows_b[...], sel_b[...], precision=high, preferred_element_type=F32)
-        at_row = lax.broadcasted_iota(jnp.int32, (24, 128), 0)
-        at_lane = lax.broadcasted_iota(jnp.int32, (24, 128), 1)
-        own_f = own.astype(F32)
-        for q in range(2):
-            spot = jnp.logical_and(at_row == 18, at_lane == 32 + q)
-            grads += jnp.where(spot, jnp.sum(own_f[q * BLK : (q + 1) * BLK]), 0.0)
-        gsec[...] = grads
-
-    arrived(krecv, k_r)
-    low_rows = lax.broadcasted_iota(jnp.int32, (8, MR), 0) < 4
-    low_lanes = lax.broadcasted_iota(jnp.int32, (8, 128), 1) < 64
-
-    def pick(values, index):
-        return jnp.take_along_axis(values, index, axis=1, mode="promise_in_bounds")
-
-    def expand(s, _):
-        got = krecv[s].astype(F32)
-        halves = []
-        for zhi in range(2):
-            first = pos[pl.ds(s * 4 + 2 * zhi, 1), :]
-            second = pos[pl.ds(s * 4 + 2 * zhi + 1, 1), :]
-            index = jnp.where(
-                low_rows,
-                jnp.broadcast_to(first, (8, MR)),
-                jnp.broadcast_to(second, (8, MR)),
-            )
-            at = [index[:, j * 128 : (j + 1) * 128] for j in range(5)]
-            re, im = got[0:8], got[8:16]
-            halves.append(
-                jnp.concatenate(
-                    [
-                        pick(re, at[0]),
-                        pick(re, at[1]),
-                        jnp.where(low_lanes, pick(re, at[2]), pick(im, at[2])),
-                        pick(im, at[3]),
-                        pick(im, at[4]),
-                    ],
-                    axis=1,
-                )
-            )
-        ex[pl.ds(pl.multiple_of(s * 16, 16), 16), :] = jnp.concatenate(halves, axis=0).astype(BF)
-        return 0
-
-    lax.fori_loop(0, NS, expand, 0, unroll=2)
-
-    def k_y(g, _):
-        rows = pl.ds(pl.multiple_of(g * 256, 256), 256)
-        half = mm(ex[rows, :], ty[...]).astype(BF).astype(F32)
-        for j in range(5):
-            hsc[j, rows, :] = half[:, j * 128 : (j + 1) * 128]
-        return 0
-
-    lax.fori_loop(0, 4, k_y, 0)
-    for j in range(NCH):
-        to_image(0, j)
-        coil_send(0, j)
-
-    def take_cot(n):
-        lo, hi = GROUPS[n]
-        arrived(crecv[n], c_r.at[n])
-        for j in range(lo, hi):
-            lanes = slice((j - lo) * 128, (j - lo + 1) * 128)
-            hsc[j] = crecv[n][:, :, lanes].astype(F32).reshape(16 * NS, 128)
-            to_image(1, j)
-            coil_send(1, j)
-
-    take_cot(0)
+
     coil_sum(0, 0)
     coil_sum(0, 1)
+    take_cot(0)
     take_cot(1)
-    windows(0)
-    into_hidden(0, w1b)
+    take_cot(2)
+    coil_sum(1, 0)
+    for step in range(2):
+        windows(0, step)
+        into_hidden(0, w1b, step)
 
     def activate(g, _):
         rows = pl.ds(pl.multiple_of(g * 16, 16), 16)
@@ -549,19 +566,46 @@
         return 0
 
     lax.fori_loop(0, MR // 16, activate, 0)
-    regularized = out_of_hidden(act, w2b)
-    for q in range(2):
-        for blk in range(NB):
-            block = regularized[q * BLK : (q + 1) * BLK, blk * 128 : (blk + 1) * 128] + b2_ref[q]
-            agsend[0, q, blk * BLK : (blk + 1) * BLK, :] = block.astype(BF)
-    gather_send(0)
-
-    coil_sum(1, 0)
-    take_cot(2)
+    for step, (lo, hi) in enumerate(BLOCKS):
+        regularized = out_of_hidden(act, w2b, step)
+        for q in range(2):
+            for blk in range(lo, hi):
+                lanes = slice((blk - lo) * 128, (blk - lo + 1) * 128)
+                block = regularized[q * BLK : (q + 1) * BLK, lanes] + b2_ref[q]
+                agsend[0, q, blk * BLK : (blk + 1) * BLK, :] = block.astype(BF)
+        gather_send(0, step)
+
     coil_sum(1, 1)
     second_grad()
 
-    arrived(agrecv.at[0], ag_r.at[0])
+    def grad_blocks(step):
+        lo, hi = BLOCKS[step]
+        windows(1, step)
+        into_hidden(1, w2f, step)
+
+        def grad_hidden(g, _):
+            rows = pl.ds(pl.multiple_of(g * 16, 16), 16)
+            kind = edge[rows, :]
+            for x3 in range(3):
+                for blk in range(lo, hi):
+                    lanes = slice((x3 * NB + blk) * 128, (x3 * NB + blk + 1) * 128)
+                    value = hid[1, rows, lanes] * hid[0, rows, lanes]
+                    gp[rows, lanes] = keep(value, kind, x3, blk).astype(BF)
+            return 0
+
+        lax.fori_loop(0, MR // 16, grad_hidden, 0, unroll=2)
+        grad_comb = out_of_hidden(gp, w1f, step)
+        for q in range(2):
+            for blk in range(lo, hi):
+                lanes = slice((blk - lo) * 128, (blk - lo + 1) * 128)
+                block = grad_comb[q * BLK : (q + 1) * BLK, lanes]
+                agsend[1, q, blk * BLK : (blk + 1) * BLK, :] = block.astype(BF)
+        gather_send(1, step)
+
+    grad_blocks(0)
+    grad_blocks(1)
+
+    gathered(0)
 
     def quarters(g):
         for half_y in range(2):
@@ -582,28 +626,6 @@
                 regpart[0, c, dst, lo] = k0 * r0 + k1 * r1
                 regpart[1, c, dst, lo] = k1 * r0 - k0 * r1
         return 0
-
-    lax.fori_loop(0, 10, begin, 0)
-    windows(1)
-    into_hidden(1, w2f)
-
-    def grad_hidden(g, _):
-        rows = pl.ds(pl.multiple_of(g * 16, 16), 16)
-        kind = edge[rows, :]
-        for x3 in range(3):
-            for blk in range(NB):
-                lanes = slice((x3 * NB + blk) * 128, (x3 * NB + blk + 1) * 128)
-                value = hid[1, rows, lanes] * hid[0, rows, lanes]
-                gp[rows, lanes] = keep(value, kind, x3, blk).astype(BF)
-        return 0
-
-    lax.fori_loop(0, MR // 16, grad_hidden, 0)
-    grad_comb = out_of_hidden(gp, w1f)
-    for q in range(2):
-        for blk in range(NB):
-            block = grad_comb[q * BLK : (q + 1) * BLK, blk * 128 : (blk + 1) * 128]
-            agsend[1, q, blk * BLK : (blk + 1) * BLK, :] = block.astype(BF)
-    gather_send(1)
 
     rows_a[...] = jnp.zeros((24, MR), F32)
     gp_mid = gp[:, LN : 2 * LN]
@@ -643,10 +665,14 @@
             total += buf[j]
         return total
 
+    grads = grads[0:8] + pltpu.roll(grads[8:16], 36, 1) + pltpu.roll(grads[16:24], 72, 1)
     grads_in = [grads]
     share(0, ar1, 16, row_zc, lambda to: (row_y * 16 + to, co))
 
-    arrived(agrecv.at[1], ag_r.at[1])
+    lax.fori_loop(0, 10, begin, 0)
+    grads_in.append(collect(0, ar1, 16))
+    share(1, ar2, 16, row_y * 4 + co, lambda to: (to // 4 * 16 + row_zc, to % 4))
+    gathered(1)
 
     def result(half):
         def finish(g, _):
@@ -674,8 +700,6 @@
 
     result(0)
 
-    grads_in.append(collect(0, ar1, 16))
-    share(1, ar2, 16, row_y * 4 + co, lambda to: (to // 4 * 16 + row_zc, to % 4))
     result(1)
     gw_ref[...] = collect(1, ar2, 16) * (1.0 / math.sqrt(NS * NY * NZ))
 
@@ -686,7 +710,9 @@
         for step, (first, count) in enumerate(STEPS):
             arrived(rsrecv.at[n, pl.ds(0, 3), :, pl.ds(first, count)], rs_s.at[n, step])
             arrived(hrecv.at[n, pl.ds(0, 4), :, pl.ds(first, count)], h_s.at[n, step])
-        arrived(agrecv.at[n, pl.ds(0, NCOIL - 1)], ag_s.at[n])
+        for step, (lo, hi) in enumerate(BLOCKS):
+            piece = agrecv.at[n, pl.ds(0, NCOIL - 1), :, pl.ds(lo * BLK, (hi - lo) * BLK)]
+            arrived(piece, ag_s.at[n, step])
     arrived(ar1.at[pl.ds(0, 15)], ar_s.at[0])
     arrived(ar2.at[pl.ds(0, 15)], ar_s.at[1])
     for p in range(2):
@@ -700,13 +726,15 @@
     stores = [pltpu.make_async_copy(held.at[s], out_hbm.at[s], sem_out.at[s]) for s in spots]
     for load in loads:
         load.start()
-    second = pltpu.roll(gw_ref[...], 96, 1)
+    folded = gw_ref[...]
+    first = jnp.concatenate([folded, pltpu.roll(folded, 92, 1), pltpu.roll(folded, 56, 1)], axis=0)
+    second = pltpu.roll(first, 128 - CH, 1)
     for a in range(3):
         for b in range(3):
             at = (a * 3 + b) * 2
-            g1_ref[a, b] = gw_ref[at : at + 2, 0:CH]
+            g1_ref[a, b] = first[at : at + 2, 0:CH]
             g2_ref[a, b] = second[at : at + 2, 0:CH]
-    gb1_ref[...] = gw_ref[18:19, 0:CH]
+    gb1_ref[...] = first[18:19, 0:CH]
     gb2_ref[...] = second[18:19, 0:2]
     for load, store in zip(loads, stores):
         load.wait()
@@ -759,8 +787,8 @@
         pltpu.VMEM((24, MR), F32),
         pltpu.VMEM((24, MR), F32),
         pltpu.VMEM((24, 128), F32),
-        pltpu.VMEM((16, 24, 128), F32),
-        pltpu.VMEM((16, 24, 128), F32),
+        pltpu.VMEM((16, 8, 128), F32),
+        pltpu.VMEM((16, 8, 128), F32),
         pltpu.VMEM((NZ, 128), jnp.int32),
         pltpu.VMEM((NZ, 128), jnp.int32),
         pltpu.VMEM((2, 128, 128), F32),
@@ -775,8 +803,8 @@
         dma((2, 2)),
         dma((2, 2)),
         dma((2, 2)),
-        dma((2,)),
-        dma((2,)),
+        dma((2, 2)),
+        dma((2, 2)),
         dma((2,)),
         dma((2,)),
     ]
@@ -785,7 +813,7 @@
         cascade_kernel,
         out_shape=(
             jax.ShapeDtypeStruct((2, CL, NY, NZ), BF),
-            jax.ShapeDtypeStruct((24, 128), F32),
+            jax.ShapeDtypeStruct((8, 128), F32),
         ),
         in_specs=[anym] * 3 + [vm] * 3 + [smem] * 2 + [anym] * len(constants),
         out_specs=(anym, vm),

time: 87.8 us -> 78.8 us (0.90)
  Pallas kernels: 86.8 us -> 77.8 us
    pallas_call x1, Pallas kernels: 83.3 us -> 74.3 us  [on_device(): pl.pallas_call(cascade_kernel, out_shape=(jax.ShapeDtypeStruct((2, CL, NY...]
where the time goes in v3:
time: 78.8 us; the launch traced here: 78.6 us
  Pallas kernels  77.8 us (99%)
  between operations  0.8 us (1%)
    pallas_call x1, Pallas kernels, on_device(): pl.pallas_call(cascade_kernel, out_shape=(jax.ShapeDtypeStruct((2, CL, NY...  74.3 us
    pallas_call x1, Pallas kernels, on_device(): pl.pallas_call(final_kernel, out_shape=(jax.ShapeDtypeStruct((2, CL, NY,...  3.49 us

profile of v3, /device:TPU:1, one launch (start us, length us, event | category | flops | bytes accessed | tf_op | source)
XLA Modules:
  0.0 78.6 jit_solution(11613149251426146338)
XLA Ops:
  0.6 74.3 %shard_map.245 = (bf16[2,4,320,256]{3,2,1,0:T(8,128)(2,1)}, f32[8,128]{1,0:T(8,128)}) custom-call(bf16[2,4,4,64,320]{4,3,2,1,0:T(8,128)(2,1)} %refs_0_.1, bf16[2,4,4,64,320]{4,3,2,1,0:T(8,128)(2,1)} %refs_1_.1, bf16[2,4,320,256]{3,2,1,0:T(8,128)(2,1)} %bitcast.15, s32[40,256]{1,0:T(8,128)} %bitcast.16, bf16[3,3,2,18]{3,2,1,0:T(2,128)(2,1)} %bitcast.17, ...), custom_call_target="tpu_custom_call" | custom-call | tf_op jit(solution)/shard_map/pallas_call | solution.py:812
  75.0 3.5 %shard_map.246 = (bf16[2,4,320,256]{3,2,1,0:T(8,128)(2,1)}, f32[3,3,2,18]{3,2,1,0:T(2,128)}, f32[1,18]{1,0:T(1,128)}, f32[3,3,2,18]{3,2,1,0:T(2,128)}, f32[1,2]{1,0:T(1,128)}) custom-call(bf16[2,4,320,256]{3,2,1,0:T(8,128)(2,1)} %get-tuple-element.12.pre_hbm, f32[8,128]{1,0:T(8,128)} %get-tuple-element.13.gw_ref), custom_call_target="tpu_custom_call" | custom-call | tf_op jit(solution)/shard_map/pallas_call | solution.py:825

commit v4 on v3

--- a/solution.py
+++ b/solution.py
@@ -22,7 +22,7 @@
 TR = 192
 LN = NB * 128
 NCH = 5
-GROUPS = ((0, 2), (2, 4), (4, 5))
+GROUPS = ((0, 4), (4, 5))
 PIECES = (
     (0, 0, 0, 64, 0),
     (1, 0, 64, 48, 0),
@@ -127,24 +127,35 @@
 
 def cascade_kernel(*refs):
     n_const = 14
-    k_hbm, cot_hbm, sens_hbm, index_ref, first_ref, second_ref, b1_ref, b2_ref = refs[:8]
+    k_hbm, cot_hbm, sens_hbm, index_hbm, first_hbm, second_hbm, b1_ref, b2_ref = refs[:8]
     const_hbm = refs[8 : 8 + n_const]
     pre_hbm, gw_ref = refs[8 + n_const : 10 + n_const]
     rest = refs[10 + n_const :]
     consts = rest[:n_const]
     (
-        kv, cv, sv, ksc, ksend, krecv, csc, cs0, cs1, cs2, cr0, cr1, cr2, pos, ex, hsc,
+        kv, cv, sv, ksc, ksend, krecv, csc, cs0, cs1, cr0, cr1, pos, ex, hsc,
         img, part, rsrecv, hrecv, tmp, vbuf, hid, act, gp, bcol,
-        w1b, w2f, w2b, w1f, agsend, agrecv, regpart, outv, rows_a, rows_b, gsec, ar1, ar2, lines_ref, lines2_ref, wt,
+        w1b, w2f, w2b, w1f, agsend, agrecv, regpart, outv, rows_a, rows_b, gsec, ar1, ar2, index_ref, first_ref, second_ref, lines_ref, lines2_ref, wt,
         ld_sem, c_ld, o_sem, k_s, k_r, c_s, c_r, rs_s, rs_r, h_s, h_r, ag_s, ag_r, ar_s, ar_r,
     ) = rest[n_const:]
     (ty, tz, spread, spread_t, pick1, pick2, rowpick, gap1, gap2, gap3, sel_a, sel_b, middle, edge) = consts
 
-    csend, crecv = (cs0, cs1, cs2), (cr0, cr1, cr2)
+    csend, crecv = (cs0, cs1), (cr0, cr1)
     me = lax.axis_index("space")
     co = lax.axis_index("coil")
     hz = co // 2
     hy = co % 2
+
+    load_i = pltpu.make_async_copy(index_hbm, index_ref, ld_sem.at[3])
+    load_w = [
+        pltpu.make_async_copy(first_hbm, first_ref, ld_sem.at[4]),
+        pltpu.make_async_copy(second_hbm, second_ref, ld_sem.at[5]),
+    ]
+    load_k = pltpu.make_async_copy(k_hbm, kv, ld_sem.at[0])
+    load_c = pltpu.make_async_copy(cot_hbm, cv, ld_sem.at[1])
+    load_s = pltpu.make_async_copy(sens_hbm, sv, ld_sem.at[2])
+    load_i.start()
+    load_k.start()
 
     barrier = pltpu.get_barrier_semaphore()
 
@@ -154,7 +165,7 @@
         )
         return 0
 
-    lax.fori_loop(1, NS, greet, 0)
+    lax.fori_loop(1, NS, greet, 0, unroll=9)
     for j in range(1, NCOIL):
         pl.semaphore_signal(
             barrier, inc=1, device_id=(me, lax.rem(co + j, NCOIL)), device_id_type=MESH
@@ -164,11 +175,10 @@
         for jc in range(1, NCOIL):
             there = (lax.rem(row_y + jy, 4) * 16 + row_zc, lax.rem(co + jc, NCOIL))
             pl.semaphore_signal(barrier, inc=1, device_id=there, device_id_type=MESH)
-    load_k = pltpu.make_async_copy(k_hbm, kv, ld_sem.at[0])
-    load_c = pltpu.make_async_copy(cot_hbm, cv, ld_sem.at[1])
-    load_s = pltpu.make_async_copy(sens_hbm, sv, ld_sem.at[2])
-    load_k.start()
+
     load_c.start()
+    for load in load_w:
+        load.start()
     loads = [
         pltpu.make_async_copy(src, dst, c_ld.at[n])
         for n, (src, dst) in enumerate(zip(const_hbm, consts))
@@ -177,6 +187,7 @@
         load.start()
     load_s.start()
 
+    load_i.wait()
     turned = jnp.concatenate(
         [index_ref[...].astype(F32), jnp.full((128 - LINES, NZ), -1.0, F32)], axis=0
     )
@@ -221,7 +232,7 @@
             ).start()
             return 0
 
-        lax.fori_loop(1, NS, send, 0)
+        lax.fori_loop(1, NS, send, 0, unroll=3)
 
     pl.semaphore_wait(barrier, NS - 1 + NCOIL - 1 + 9)
     spread_out(ksend, krecv, k_s, k_r)
@@ -268,6 +279,8 @@
     lax.fori_loop(0, NZ // 32, find, 0)
 
     load_s.wait()
+    for load in load_w:
+        load.wait()
 
     def to_image(n, j):
         columns = []
@@ -546,7 +559,6 @@
     coil_sum(0, 1)
     take_cot(0)
     take_cot(1)
-    take_cot(2)
     coil_sum(1, 0)
     for step in range(2):
         windows(0, step)
@@ -720,13 +732,17 @@
             store(p, half).wait()
 
 
-def final_kernel(pre_hbm, gw_ref, out_hbm, g1_ref, gb1_ref, g2_ref, gb2_ref, held, sem_in, sem_out):
+def final_kernel(pre_hbm, gw_hbm, out_hbm, g1_hbm, gb1_hbm, g2_hbm, gb2_hbm, *scratch):
+    held, folded_ref, g1_ref, gb1_ref, g2_ref, gb2_ref, sem_in, sem_out, sem_small = scratch
+    load_g = pltpu.make_async_copy(gw_hbm, folded_ref, sem_small.at[4])
+    load_g.start()
     spots = [(p, c) for p in range(2) for c in range(CL)]
     loads = [pltpu.make_async_copy(pre_hbm.at[s], held.at[s], sem_in.at[s]) for s in spots]
     stores = [pltpu.make_async_copy(held.at[s], out_hbm.at[s], sem_out.at[s]) for s in spots]
     for load in loads:
         load.start()
-    folded = gw_ref[...]
+    load_g.wait()
+    folded = folded_ref[...]
     first = jnp.concatenate([folded, pltpu.roll(folded, 92, 1), pltpu.roll(folded, 56, 1)], axis=0)
     second = pltpu.roll(first, 128 - CH, 1)
     for a in range(3):
@@ -736,6 +752,10 @@
             g2_ref[a, b] = second[at : at + 2, 0:CH]
     gb1_ref[...] = first[18:19, 0:CH]
     gb2_ref[...] = second[18:19, 0:2]
+    small = [(g1_ref, g1_hbm), (gb1_ref, gb1_hbm), (g2_ref, g2_hbm), (gb2_ref, gb2_hbm)]
+    stores += [pltpu.make_async_copy(*pair, sem_small.at[n]) for n, pair in enumerate(small)]
+    for store in stores[8:]:
+        store.start()
     for load, store in zip(loads, stores):
         load.wait()
         store.start()
@@ -789,10 +809,13 @@
         pltpu.VMEM((24, 128), F32),
         pltpu.VMEM((16, 8, 128), F32),
         pltpu.VMEM((16, 8, 128), F32),
+        pltpu.VMEM((LINES, NZ), jnp.int32),
+        pltpu.VMEM((3, 3, 2, CH), BF),
+        pltpu.VMEM((3, 3, 2, CH), BF),
         pltpu.VMEM((NZ, 128), jnp.int32),
         pltpu.VMEM((NZ, 128), jnp.int32),
         pltpu.VMEM((2, 128, 128), F32),
-        dma((3,)),
+        dma((6,)),
         dma((len(constants),)),
         dma((4,)),
         dma,
@@ -815,7 +838,7 @@
             jax.ShapeDtypeStruct((2, CL, NY, NZ), BF),
             jax.ShapeDtypeStruct((8, 128), F32),
         ),
-        in_specs=[anym] * 3 + [vm] * 3 + [smem] * 2 + [anym] * len(constants),
+        in_specs=[anym] * 6 + [smem] * 2 + [anym] * len(constants),
         out_specs=(anym, vm),
         scratch_shapes=scratch,
         compiler_params=pltpu.CompilerParams(
@@ -831,9 +854,19 @@
             jax.ShapeDtypeStruct((3, 3, 2, CH), F32),
             jax.ShapeDtypeStruct((1, 2), F32),
         ),
-        in_specs=[anym, vm],
-        out_specs=(anym, vm, vm, vm, vm),
-        scratch_shapes=[pltpu.VMEM((2, CL, NY, NZ), BF), dma((2, CL)), dma((2, CL))],
+        in_specs=[anym] * 2,
+        out_specs=(anym,) * 5,
+        scratch_shapes=[
+            pltpu.VMEM((2, CL, NY, NZ), BF),
+            pltpu.VMEM((8, 128), F32),
+            pltpu.VMEM((3, 3, 2, CH), F32),
+            pltpu.VMEM((1, CH), F32),
+            pltpu.VMEM((3, 3, 2, CH), F32),
+            pltpu.VMEM((1, 2), F32),
+            dma((2, CL)),
+            dma((2, CL)),
+            dma((5,)),
+        ],
         compiler_params=pltpu.CompilerParams(vmem_limit_bytes=60 * 1024 * 1024),
     )(result, grads)
     grad_sens = jnp.transpose(grad_sens, (0, 1, 3, 2)).reshape(2, CL, NZ, 1, NY)

time: 78.8 us -> 77.4 us (0.982)
  Pallas kernels: 77.8 us -> 76.4 us
    pallas_call x1, Pallas kernels: 3.49 us -> 2.52 us  [on_device(): pl.pallas_call(final_kernel, out_shape=(jax.ShapeDtypeStruct((2, CL, NY,...]
where the time goes in v4:
time: 77.4 us; the launch traced here: 77.2 us
  Pallas kernels  76.4 us (99%)
  between operations  0.8 us (1%)
    pallas_call x1, Pallas kernels, on_device(): pl.pallas_call(cascade_kernel, out_shape=(jax.ShapeDtypeStruct((2, CL, NY...  73.9 us
    pallas_call x1, Pallas kernels, on_device(): pl.pallas_call(final_kernel, out_shape=(jax.ShapeDtypeStruct((2, CL, NY,...  2.52 us

profile of v4, /device:TPU:1, one launch (start us, length us, event | category | flops | bytes accessed | tf_op | source)
XLA Modules:
  0.0 77.2 jit_solution(7131867230096145340)
XLA Ops:
  0.6 73.9 %shard_map.245 = (bf16[2,4,320,256]{3,2,1,0:T(8,128)(2,1)}, f32[8,128]{1,0:T(8,128)}) custom-call(bf16[2,4,4,64,320]{4,3,2,1,0:T(8,128)(2,1)} %refs_0_.1, bf16[2,4,4,64,320]{4,3,2,1,0:T(8,128)(2,1)} %refs_1_.1, bf16[2,4,320,256]{3,2,1,0:T(8,128)(2,1)} %bitcast.15, s32[40,256]{1,0:T(8,128)} %bitcast.16, bf16[3,3,2,18]{3,2,1,0:T(2,128)(2,1)} %bitcast.17, ...), custom_call_target="tpu_custom_call" | custom-call | tf_op jit(solution)/shard_map/pallas_call | solution.py:835
  74.5 2.5 %shard_map.246 = (bf16[2,4,320,256]{3,2,1,0:T(8,128)(2,1)}, f32[3,3,2,18]{3,2,1,0:T(2,128)}, f32[1,18]{1,0:T(1,128)}, f32[3,3,2,18]{3,2,1,0:T(2,128)}, f32[1,2]{1,0:T(1,128)}) custom-call(bf16[2,4,320,256]{3,2,1,0:T(8,128)(2,1)} %get-tuple-element.12.pre_hbm, f32[8,128]{1,0:T(8,128)} %get-tuple-element.13.gw_hbm), custom_call_target="tpu_custom_call" | custom-call | tf_op jit(solution)/shard_map/pallas_call | solution.py:848

commit v5 on v4

--- a/solution.py
+++ b/solution.py
@@ -89,8 +89,6 @@
     for r, _, v in hid:
         inner[r] = 1 <= v <= BLK
     gap3 = np.where(inner[None, :], gap1.T, 99.0).astype(np.float32)
-    sel_a = spread
-    sel_b = np.roll(spread, CH, axis=1)
     middle = np.broadcast_to(inner[None, :], (8, MR)).astype(np.float32)
     edge = np.zeros((MR, 128), np.float32)
     for r, _, v in hid:
@@ -106,8 +104,6 @@
         gap1,
         gap2,
         gap3,
-        sel_a,
-        sel_b,
         middle,
         edge,
     ]
@@ -126,7 +122,7 @@
 
 
 def cascade_kernel(*refs):
-    n_const = 14
+    n_const = 12
     k_hbm, cot_hbm, sens_hbm, index_hbm, first_hbm, second_hbm, b1_ref, b2_ref = refs[:8]
     const_hbm = refs[8 : 8 + n_const]
     pre_hbm, gw_ref = refs[8 + n_const : 10 + n_const]
@@ -138,7 +134,7 @@
         w1b, w2f, w2b, w1f, agsend, agrecv, regpart, outv, rows_a, rows_b, gsec, ar1, ar2, index_ref, first_ref, second_ref, lines_ref, lines2_ref, wt,
         ld_sem, c_ld, o_sem, k_s, k_r, c_s, c_r, rs_s, rs_r, h_s, h_r, ag_s, ag_r, ar_s, ar_r,
     ) = rest[n_const:]
-    (ty, tz, spread, spread_t, pick1, pick2, rowpick, gap1, gap2, gap3, sel_a, sel_b, middle, edge) = consts
+    (ty, tz, spread, spread_t, pick1, pick2, rowpick, gap1, gap2, gap3, middle, edge) = consts
 
     csend, crecv = (cs0, cs1), (cr0, cr1)
     me = lax.axis_index("space")
@@ -416,6 +412,13 @@
     def gathered(n):
         for step, (lo, hi) in enumerate(BLOCKS):
             arrived(agrecv.at[n, :, :, pl.ds(lo * BLK, (hi - lo) * BLK)], ag_r.at[n, step])
+
+    def group_sums(rows):
+        high = rows.astype(BF)
+        rest_of = rows - high.astype(F32)
+        middle_part = rest_of.astype(BF)
+        low = (rest_of - middle_part.astype(F32)).astype(BF)
+        return mm(high, spread[...]) + mm(middle_part, spread[...]) + mm(low, spread[...])
 
     def second_grad():
         rows_b[...] = jnp.zeros((24, MR), F32)
@@ -443,8 +446,7 @@
                         axis=0,
                         keepdims=True,
                     )
-        high = lax.Precision.HIGHEST
-        grads = jnp.dot(rows_b[...], sel_b[...], precision=high, preferred_element_type=F32)
+        grads = pltpu.roll(group_sums(rows_b[...]), CH, 1)
         at_row = lax.broadcasted_iota(jnp.int32, (24, 128), 0)
         at_lane = lax.broadcasted_iota(jnp.int32, (24, 128), 1)
         own_f = own.astype(F32)
@@ -558,11 +560,11 @@
     coil_sum(0, 0)
     coil_sum(0, 1)
     take_cot(0)
-    take_cot(1)
-    coil_sum(1, 0)
     for step in range(2):
         windows(0, step)
         into_hidden(0, w1b, step)
+    take_cot(1)
+    coil_sum(1, 0)
 
     def activate(g, _):
         rows = pl.ds(pl.multiple_of(g * 16, 16), 16)
@@ -654,8 +656,7 @@
                 )
     sums = mm_nt(jnp.ones((8, LN), BF), gp_mid) * middle[...]
     rows_a[18:19, :] = sums[0:1, :]
-    high = lax.Precision.HIGHEST
-    grads = jnp.dot(rows_a[...], sel_a[...], precision=high, preferred_element_type=F32)
+    grads = group_sums(rows_a[...])
     grads += gsec[...]
     def share(n, buf, count, mine, device):
         buf[mine] = grads_in[n]

time: 77.4 us -> 76.9 us (level)
  no operation moved by 1% of the time
where the time goes in v5:
time: 76.9 us; the launch traced here: 76.8 us
  Pallas kernels  76 us (99%)
  between operations  0.8 us (1%)
    pallas_call x1, Pallas kernels, on_device(): pl.pallas_call(cascade_kernel, out_shape=(jax.ShapeDtypeStruct((2, CL, NY...  73.5 us
    pallas_call x1, Pallas kernels, on_device(): pl.pallas_call(final_kernel, out_shape=(jax.ShapeDtypeStruct((2, CL, NY,...  2.52 us

profile of v5, /device:TPU:1, one launch (start us, length us, event | category | flops | bytes accessed | tf_op | source)
XLA Modules:
  0.0 76.8 jit_solution(14070685202349601804)
XLA Ops:
  0.6 73.5 %shard_map.227 = (bf16[2,4,320,256]{3,2,1,0:T(8,128)(2,1)}, f32[8,128]{1,0:T(8,128)}) custom-call(bf16[2,4,4,64,320]{4,3,2,1,0:T(8,128)(2,1)} %refs_0_.1, bf16[2,4,4,64,320]{4,3,2,1,0:T(8,128)(2,1)} %refs_1_.1, bf16[2,4,320,256]{3,2,1,0:T(8,128)(2,1)} %bitcast.15, s32[40,256]{1,0:T(8,128)} %bitcast.16, bf16[3,3,2,18]{3,2,1,0:T(2,128)(2,1)} %bitcast.17, ...), custom_call_target="tpu_custom_call" | custom-call | tf_op jit(solution)/shard_map/pallas_call | solution.py:836
  74.1 2.5 %shard_map.228 = (bf16[2,4,320,256]{3,2,1,0:T(8,128)(2,1)}, f32[3,3,2,18]{3,2,1,0:T(2,128)}, f32[1,18]{1,0:T(1,128)}, f32[3,3,2,18]{3,2,1,0:T(2,128)}, f32[1,2]{1,0:T(1,128)}) custom-call(bf16[2,4,320,256]{3,2,1,0:T(8,128)(2,1)} %get-tuple-element.12.pre_hbm, f32[8,128]{1,0:T(8,128)} %get-tuple-element.13.gw_hbm), custom_call_target="tpu_custom_call" | custom-call | tf_op jit(solution)/shard_map/pallas_call | solution.py:849
